TPU v7x, 32 devices: a whole 2x2x4 slice. The times are simulated.
32 devices in a mesh: dp: 16 (over z, y, x), sp: 2 (over core).
Axes of the slice: x: 2, y: 2, z: 4, core: 2. Of those that a mesh axis runs over, the one named last changes fastest.
Arguments:
- tokens_in: bfloat16 [16, 512, 1152], P('dp', 'sp'), may hold values from -6 to 6
- segment_ids: int32 [16, 512], P('dp', 'sp'), may hold values from 0 to 3, as said below
- conditions: bfloat16 [16, 4, 1152], P('dp'), may hold values from -6 to 6
- noise_bins: int32 [16, 4], P('dp'), may hold values from 0 to 7
- bin_counts: int32 [16, 8], P('dp'), may hold values from 10 to 90
- cotangent: bfloat16 [16, 512, 1152], P('dp', 'sp'), may hold values from -6 to 6
- ada_weight: bfloat16 [1152, 6912], P(('dp', 'sp')), may hold values from -0.1875 to 0.1875
- qkv_weight: bfloat16 [1152, 3456], P(('dp', 'sp')), may hold values from -0.1875 to 0.1875
- out_weight: bfloat16 [1152, 1152], P(('dp', 'sp')), may hold values from -1.75 to 1.75
- up_weight: bfloat16 [1152, 4608], P(('dp', 'sp')), may hold values from -0.1875 to 0.1875
- down_weight: bfloat16 [4608, 1152], P(('dp', 'sp')), may hold values from -0.09375 to 0.09375
Outputs:
- tokens_out: bfloat16 [16, 512, 1152], P('dp', 'sp')
- tokens_grad: float32 [16, 512, 1152], P('dp', 'sp')
- cond_grad: float32 [16, 4, 1152], P('dp')
- ada_grad: float32 [1152, 6912], P(('dp', 'sp'))
- qkv_grad: float32 [1152, 3456], P(('dp', 'sp'))
- out_grad: float32 [1152, 1152], P(('dp', 'sp'))
- up_grad: float32 [1152, 4608], P(('dp', 'sp'))
- down_grad: float32 [4608, 1152], P(('dp', 'sp'))
Inputs may be any that keep to these rules, and one draw needn't show every extreme that they name: `segment_ids`: within each sequence the crop numbers never fall, each of 0 to 3 holds one token or more, and the crop that holds position 256 also holds position 255.
All inputs are finite; a program needn't handle non-finite values.
Results may differ from a plain program's by a relative error of at most 0.012.
The roundings to bfloat16 on the way count: a program that leaves them out, or rounds other values in their place, can miss the bound.
Values may be sent and summed in bfloat16 or wider, within the bound.
A program may use at most 384 MiB of HBM per device.

v0:
```python
from functools import partial
import math

import jax
import jax.numpy as jnp
from jax import lax
from jax.experimental import pallas as pl
from jax.experimental.pallas import tpu as pltpu
from jax.sharding import PartitionSpec as P

HEADS = 16
CROPS = 4
NBINS = 8
EPSILON = 1e-06
LARGE_NEGATIVE = -1e30
GELU_SCALE = math.sqrt(2.0 / math.pi)
GELU_CUBE = 0.044715

MESH = pl.DeviceIdType.MESH
PAD = 48
CUT = 80
CHIPS = 16
BAND = 1792
PLACES = ((0, 0), (0, 1), (1, 0), (1, 1))


def position():
    d = lax.axis_index("dp")
    c = lax.axis_index("sp")
    return d // 4, (d // 2) % 2, d % 2, c


def device(z, y, x, c):
    return (z * 4 + y * 2 + x, c)


def block_of(kind, zy, group):
    if kind == 2:
        return zy // 2, (zy % 2) * 4 + group
    return group, zy


def greet(peers):
    barrier = pltpu.get_barrier_semaphore()
    for peer in peers:
        pl.semaphore_signal(barrier, inc=1, device_id=peer, device_id_type=MESH)
    pl.semaphore_wait(barrier, len(peers))


def remote(src, dst, send, recv, target):
    return pltpu.make_async_remote_copy(
        src_ref=src,
        dst_ref=dst,
        send_sem=send,
        recv_sem=recv,
        device_id=target,
        device_id_type=MESH,
    )


def arrive(ref, sem, target):
    remote(ref, ref, sem, sem, target).wait_recv()


def row_selector(rows, share):
    shape = (rows, 4 * PAD)
    row = lax.broadcasted_iota(jnp.int32, shape, 0)
    column = lax.broadcasted_iota(jnp.int32, shape, 1)
    picked = jnp.zeros(shape, jnp.bool_)
    for k in range(4):
        inside = (row >= k * share) & (row < (k + 1) * share)
        picked = picked | (inside & (column == row - k * share + k * PAD))
    return picked.astype(jnp.float32).astype(jnp.bfloat16)


def product(left, right):
    return jnp.dot(left, right, preferred_element_type=jnp.float32)


def product_by_rows(left, right):
    return lax.dot_general(left, right, (((0,), (0,)), ((), ())), preferred_element_type=jnp.float32)


def product_by_columns(left, right):
    return lax.dot_general(left, right, (((1,), (1,)), ((), ())), preferred_element_type=jnp.float32)


def chunks(rows, body, step=16):
    def run(i, carry):
        body(pl.ds(pl.multiple_of(i * step, step), step))
        return carry

    lax.fori_loop(0, rows // step, run, 0)


def normed(values):
    center = values - jnp.mean(values, axis=-1, keepdims=True)
    inverse = lax.rsqrt(jnp.mean(center * center, axis=-1, keepdims=True) + EPSILON)
    return center * inverse, inverse


def pick(segments, table, first, column, width):
    columns = slice(column * width, (column + 1) * width)
    value = table[first + 3 : first + 4, columns]
    for crop in (2, 1, 0):
        value = jnp.where(segments == crop, table[first + crop : first + crop + 1, columns], value)
    return value


def window_of(head, size, width):
    start = jnp.minimum((head * size) // 128, width // 128 - 2) * 128
    start = pl.multiple_of(start, 128)
    lane = lax.broadcasted_iota(jnp.int32, (1, 256), 1) + start
    return pl.ds(start, 256), (lane >= head * size) & (lane < (head + 1) * size)


def forward_kernel(share, shards_ref, down_ref, act_ref, ada_ref, tokens_ref, cot_ref, seg_col_ref,
                   seg_row_ref, bins_ref,
                   weights_ref, down_part_ref, slope_ref, hidden_ref, query_ref, sides_ref, total_ref,
                   context_ref, attended_ref, middle_ref, hidden_two_ref, mlp_ref, out_ref, table_ref,
                   conds_ref, level_ref,
                   full, stage, part, part_recv, band, band_diag, band_x, band_y, band_z, halves_of,
                   seg_all, bias, work, active, grad_mlp, slope, *sems):
    (
        group_send, group_recv, z_send, z_recv, x_send, x_recv, y_send, y_recv,
        dx_send, dx_recv, dy_send, dy_recv, c_send, c_recv,
        cond_send, cond_recv, pc_send, pc_recv, pd_send, pd_recv, px_send, px_recv, py_send, py_recv,
        pz_send, pz_recv, pm_send, pm_recv, seg_send, seg_recv, kv_send, kv_recv,
        save_sem, grad_sem, slope_sem,
    ) = sems
    z, y, x, c = position()
    me = z * 4 + y * 2 + x
    group = x * 2 + c
    zy = z * 2 + y
    rows = 4 * share
    count, width = tokens_ref.shape
    halves = (pl.ds(0, CUT), pl.ds(CUT, rows - CUT))
    x_peer, y_peer, c_peer = device(z, y, 1 - x, c), device(z, 1 - y, x, c), device(z, y, x, 1 - c)
    partners = [(x, 1 - c), (1 - x, c), (1 - x, 1 - c)]
    greet(
        [((me + k) % CHIPS, c) for k in range(1, CHIPS)] + [c_peer, device(z, y, 1 - x, 1 - c)]
    )
    sends = {a: [] for a in (0, 1, 2, "other")}

    def send(a, *args):
        copy = remote(*args)
        copy.start()
        sends[a].append(copy)

    def finish_sends(a):
        for copy in sends[a]:
            copy.wait_send()
        sends[a] = []

    def place(a, k, other_y, other_x, core=None):
        zz = (z - k + 4) % 4
        yy = 1 - y if other_y else y
        xx = 1 - x if other_x else x
        cc = c if core is None else core
        block, row = block_of(a, zz * 2 + yy, xx * 2 + cc)
        return full.at[a, block, pl.ds(pl.multiple_of(row * rows, 16), rows)]

    def half(a, k, other_y, other_x, h):
        zz = (z - k + 4) % 4
        yy = 1 - y if other_y else y
        xx = 1 - x if other_x else x
        block, row = block_of(a, zz * 2 + yy, xx * 2 + c)
        start = row * rows + (CUT if h else 0)
        return full.at[a, block, pl.ds(pl.multiple_of(start, 16), rows - CUT if h else CUT)]

    for a in range(2):
        for j, (px, pc) in enumerate(partners):
            send(
                "other",
                shards_ref.at[a, px * 2 + pc],
                stage.at[a, pl.ds(pl.multiple_of(group * PAD, 16), PAD)],
                group_send.at[a, j],
                group_recv.at[a, j],
                device(z, y, px, pc),
            )
    for k in range(1, CHIPS):
        to = (me + k) % CHIPS
        send("other", act_ref.at[to], conds_ref.at[me], cond_send.at[k - 1], cond_recv.at[k - 1], (to, c))
    seg_all[c] = seg_row_ref[...]
    send("other", seg_row_ref, seg_all.at[c], seg_send, seg_recv, c_peer)
    conds_ref[me] = act_ref[me]
    for a in range(2):
        stage[a, pl.ds(pl.multiple_of(group * PAD, 16), PAD), :] = shards_ref[a, group]

    def own(a):
        block, row = block_of(a, zy, group)
        here = pl.ds(pl.multiple_of(row * rows, 16), rows)
        if a < 2:
            for j, (px, pc) in enumerate(partners):
                arrive(
                    stage.at[a, pl.ds(pl.multiple_of((px * 2 + pc) * PAD, 16), PAD)],
                    group_recv.at[a, j],
                    device(z, y, px, pc),
                )
            full[a, block, here, :] = product(row_selector(rows, share), stage[a]).astype(jnp.bfloat16)
        else:
            full[a, block, here, :] = down_ref[...]
        mine = place(a, 0, 0, 0)
        for k in (1, 2, 3):
            send(a, mine, mine, z_send.at[a, k - 1], z_recv.at[a, k - 1], device((z + k) % 4, y, x, c))

    def to_core(a, k, pos):
        piece = place(a, k, *PLACES[pos])
        send(a, piece, piece, c_send.at[a, k, pos], c_recv.at[a, k, pos], c_peer)

    def spread(a, k):
        if k:
            arrive(place(a, k, 0, 0), z_recv.at[a, k - 1], device((z - k + 4) % 4, y, x, c))
        for h in (0, 1):
            one, two = half(a, k, 0, 0, h), half(a, k, 0, 0, 1 - h)
            send(a, one, one, x_send.at[a, k, h], x_recv.at[a, k, h], x_peer)
            send(a, two, two, y_send.at[a, k, 1 - h], y_recv.at[a, k, 1 - h], y_peer)
        to_core(a, k, 0)

    def forward(a, k):
        top, low = half(a, k, 0, 1, 0), half(a, k, 1, 0, 1)
        arrive(top, x_recv.at[a, k, 0], x_peer)
        send(a, top, top, dy_send.at[a, k], dy_recv.at[a, k], y_peer)
        arrive(low, y_recv.at[a, k, 1], y_peer)
        send(a, low, low, dx_send.at[a, k], dx_recv.at[a, k], x_peer)
        arrive(half(a, k, 0, 1, 1), x_recv.at[a, k, 1], x_peer)
        to_core(a, k, 1)
        arrive(half(a, k, 1, 0, 0), y_recv.at[a, k, 0], y_peer)
        to_core(a, k, 2)

    def finish(a, k):
        arrive(half(a, k, 1, 1, 0), dy_recv.at[a, k], y_peer)
        arrive(half(a, k, 1, 1, 1), dx_recv.at[a, k], x_peer)
        to_core(a, k, 3)

    saves = []

    def complete(a):
        for k in range(4):
            for pos, (oy, ox) in enumerate(PLACES):
                arrive(place(a, k, oy, ox, 1 - c), c_recv.at[a, k, pos], c_peer)
        copy = pltpu.make_async_copy(full.at[a], weights_ref.at[a], save_sem.at[a])
        copy.start()
        saves.append(copy)

    def mod_start():
        for k in range(1, CHIPS):
            source = (me - k + CHIPS) % CHIPS
            arrive(conds_ref.at[source], cond_recv.at[k - 1], (source, c))
        acts = conds_ref[:, :8, :].astype(jnp.float32).reshape(CHIPS * 8, 128)
        row = lax.broadcasted_iota(jnp.int32, acts.shape, 0) % 8
        upper = jnp.where(row < CROPS, acts, 0.0).astype(jnp.bfloat16)
        lower = pltpu.roll(jnp.where(row < CROPS, acts, 0.0), CROPS, 0).astype(jnp.bfloat16)
        side = ada_ref.shape[1] // 2
        part[...] = product(upper, ada_ref[:, :side]) + product(lower, ada_ref[:, side:])
        far = pl.ds(pl.multiple_of((1 - c) * (side - BAND), 128), BAND)
        send("other", part.at[:, far], part_recv, pc_send, pc_recv, c_peer)

    def block8(zz, yy, xx):
        return pl.ds(pl.multiple_of((zz * 4 + yy * 2 + xx) * 8, 8), 8)

    def mod_cores():
        arrive(part_recv, pc_recv, c_peer)
        side = ada_ref.shape[1] // 2
        near = pl.ds(pl.multiple_of(c * (side - BAND), 128), BAND)
        band[...] = part[:, near] + part_recv[...]
        for k in range(4):
            zz = (z + k) % 4
            src = band.at[block8(zz, 1 - y, 1 - x)]
            send("other", src, band_diag.at[k], pd_send.at[k], pd_recv.at[k], x_peer if k % 2 else y_peer)

    def mod_plane():
        for k in range(4):
            zz = (z + k) % 4
            to_x, to_y = block8(zz, y, 1 - x), block8(zz, 1 - y, x)
            arrive(band_diag.at[k], pd_recv.at[k], x_peer if k % 2 else y_peer)
            fold = to_y if k % 2 else to_x
            band[fold, :] = band[fold, :] + band_diag[k]
            send("other", band.at[to_x], band_x.at[k], px_send.at[k], px_recv.at[k], x_peer)
            send("other", band.at[to_y], band_y.at[k], py_send.at[k], py_recv.at[k], y_peer)

    def mod_line():
        for k in (1, 2, 3, 0):
            zz = (z + k) % 4
            mine = block8(zz, y, x)
            arrive(band_x.at[k], px_recv.at[k], x_peer)
            arrive(band_y.at[k], py_recv.at[k], y_peer)
            band[mine, :] = band[mine, :] + band_x[k] + band_y[k]
            if k:
                send("other", band.at[mine], band_z.at[k - 1], pz_send.at[k - 1], pz_recv.at[k - 1], device(zz, y, x, c))

    def mod_last():
        for k in (1, 2, 3):
            arrive(band_z.at[k - 1], pz_recv.at[k - 1], device((z - k + 4) % 4, y, x, c))
        halves_of[c] = band[block8(z, y, x), :] + band_z[0] + band_z[1] + band_z[2]
        send("other", halves_of.at[c], halves_of.at[c], pm_send, pm_recv, c_peer)

    def mod_end():
        arrive(halves_of.at[1 - c], pm_recv, c_peer)
        side = ada_ref.shape[1] // 2
        table_ref[:, :BAND] = halves_of[0]
        table_ref[:, BAND:] = halves_of[1][:, 2 * BAND - side :]
        counts = jnp.sum(conds_ref[:, :, :].astype(jnp.float32)[:, CROPS : CROPS + 1, :], axis=0)
        lane = lax.broadcasted_iota(jnp.int32, counts.shape, 1)
        weight = jnp.where(lane < NBINS, 40.0 * CHIPS / jnp.where(lane < NBINS, counts, 1.0), 0.0)
        level_ref[...] = jnp.broadcast_to(
            jnp.sum(bins_ref[...] * weight, axis=-1, keepdims=True), level_ref.shape
        )

    def first_norm():
        def body(at):
            segments = seg_col_ref[at, :1]
            value, _ = normed(tokens_ref[at, :].astype(jnp.float32))
            value = value * (1.0 + pick(segments, table_ref, 0, 1, width))
            hidden_ref[at, :] = (value + pick(segments, table_ref, 0, 0, width)).astype(jnp.bfloat16)

        chunks(count, body)
        arrive(seg_all.at[1 - c], seg_recv, c_peer)
        for h in (0, 1):
            same = seg_col_ref[:, :1] == seg_all[h][:1, :]
            bias[:, h * count : (h + 1) * count] = jnp.where(same, 0.0, LARGE_NEGATIVE)

    def project():
        here = pl.ds(pl.multiple_of(c * count, 256), count)
        for q in (1, 2):
            sides_ref[q - 1, here, :] = product(hidden_ref[...], full[0, q]).astype(jnp.bfloat16)
            send("other", sides_ref.at[q - 1, here], sides_ref.at[q - 1, here], kv_send.at[q - 1], kv_recv.at[q - 1], c_peer)
        query_ref[...] = product(hidden_ref[...], full[0, 0]).astype(jnp.bfloat16)
        total_ref[...] = jnp.zeros_like(total_ref)
        work[...] = jnp.zeros_like(work)

    def attend(first, last):
        if first == 0:
            there = pl.ds(pl.multiple_of((1 - c) * count, 256), count)
            for q in (0, 1):
                arrive(sides_ref.at[q, there], kv_recv.at[q], c_peer)
        size = width // HEADS
        scale = 1.0 / math.sqrt(size)

        def body(head, carry):
            columns, inside = window_of(head, size, width)
            query = query_ref[:, columns]
            query = jnp.where(inside, query, jnp.zeros_like(query))
            scores = product_by_columns(query, sides_ref[0, :, columns]) * scale + bias[...]
            top = jnp.max(scores, axis=-1, keepdims=True)
            raised = jnp.exp(scores - top)
            total = jnp.sum(raised, axis=-1, keepdims=True)
            chance = (raised * (1.0 / total)).astype(jnp.bfloat16)
            context = product(chance, sides_ref[1, :, columns])
            work[:, columns] = jnp.where(inside, context, work[:, columns])
            lane = lax.broadcasted_iota(jnp.int32, (1, 128), 1)
            total_ref[...] = jnp.where(lane == head, top + jnp.log(total), total_ref[...])
            return carry

        lax.fori_loop(first, last, body, 0)

    def mix():
        context_ref[...] = work[...].astype(jnp.bfloat16)
        attended_ref[...] = product(context_ref[...], full[0, 3])

        def body(at):
            segments = seg_col_ref[at, :1]
            gate = pick(segments, table_ref, 0, 2, width)
            middle = tokens_ref[at, :].astype(jnp.float32) + gate * attended_ref[at, :]
            middle_ref[at, :] = middle
            value, _ = normed(middle)
            value = value * (1.0 + pick(segments, table_ref, 4, 1, width))
            hidden_two_ref[at, :] = (value + pick(segments, table_ref, 4, 0, width)).astype(jnp.bfloat16)
            level = level_ref[3:4, :1]
            for crop in (2, 1, 0):
                level = jnp.where(segments == crop, level_ref[crop : crop + 1, :1], level)
            grad = cot_ref[at, :].astype(jnp.float32) * level
            grad_mlp[at, :] = (grad * pick(segments, table_ref, 4, 2, width)).astype(jnp.bfloat16)

        chunks(count, body)

    slope_copies = {}

    def expand(q):
        work[...] = product(hidden_two_ref[...], full[1, q])
        if q >= 2:
            slope_copies[q - 2].wait()

        def body(at):
            u = work[at, :]
            square = u * u
            bend = jnp.tanh(GELU_SCALE * (u + GELU_CUBE * (square * u)))
            active[q, at, :] = (0.5 * u * (1.0 + bend)).astype(jnp.bfloat16)
            inner = GELU_SCALE * (1.0 + 3.0 * GELU_CUBE * square)
            slope[q % 2, at, :] = 0.5 * (1.0 + bend) + 0.5 * u * (1.0 - bend * bend) * inner

        chunks(count, body)
        copy = pltpu.make_async_copy(slope.at[q % 2], slope_ref.at[q], slope_sem.at[q % 2])
        copy.start()
        slope_copies[q] = copy

    def down_grad(q):
        if q == 0:
            finish_sends(0)
            saves[0].wait()
        full[0, q] = product_by_rows(active[q], grad_mlp[...]).astype(jnp.bfloat16)
        copy = pltpu.make_async_copy(full.at[0, q], down_part_ref.at[q], grad_sem.at[q])
        copy.start()
        saves.append(copy)

    def contract():
        work[...] = product(active[0], full[2, 0])
        for q in (1, 2, 3):
            work[...] += product(active[q], full[2, q])

        def body(at):
            mlp = work[at, :]
            mlp_ref[at, :] = mlp
            gate = pick(seg_col_ref[at, :1], table_ref, 4, 2, width)
            out_ref[at, :] = (middle_ref[at, :] + gate * mlp).astype(jnp.bfloat16)

        chunks(count, body)

    extra = {
        1: [mod_start],
        2: [mod_cores],
        3: [mod_plane],
        4: [mod_line],
        5: [mod_last],
        6: [mod_end, first_norm, partial(complete, 0), project],
        7: [partial(attend, 0, 8)],
        8: [partial(attend, 8, 16)],
        9: [mix],
        10: [partial(complete, 1), partial(expand, 0), partial(expand, 1)],
        11: [partial(expand, 2), partial(expand, 3)],
        12: [partial(down_grad, 0), partial(down_grad, 1)],
        13: [partial(down_grad, 2), partial(down_grad, 3)],
        14: [partial(complete, 2), contract],
    }
    order = [(a, k) for a in range(3) for k in range(4)]
    own(0)
    for i in range(len(order) + 3):
        if i < len(order):
            a, k = order[i]
            if k == 1 and a < 2:
                own(a + 1)
            spread(a, k)
        if 2 <= i < len(order) + 2:
            forward(*order[i - 2])
        if 3 <= i:
            finish(*order[i - 3])
        for step in extra.get(i, ()):
            step()
    for copy in saves[1:]:
        copy.wait()
    for q in (2, 3):
        slope_copies[q].wait()
    for a in (1, 2, "other"):
        finish_sends(a)


def run_forward(shards, down, acts, ada, tokens, cot, seg_col, seg_row, bins, share):
    count, width = tokens.shape
    dma = pltpu.SemaphoreType.DMA
    low, wide = jnp.bfloat16, jnp.float32
    side = ada.shape[1] // 2
    vmem, any_ = pl.BlockSpec(memory_space=pltpu.VMEM), pl.BlockSpec(memory_space=pl.ANY)
    out = jax.ShapeDtypeStruct
    return pl.pallas_call(
        partial(forward_kernel, share),
        out_shape=(
            out((3, 4, width, width), low),
            out((4, width, width), low),
            out((4, count, width), wide),
            out((count, width), low),
            out((count, width), low),
            out((2, 2 * count, width), low),
            out((count, 128), wide),
            out((count, width), low),
            out((count, width), wide),
            out((count, width), wide),
            out((count, width), low),
            out((count, width), wide),
            out((count, width), low),
            out((8, side), wide),
            out((CHIPS, 16, 128), low),
            out((8, 128), wide),
        ),
        in_specs=[vmem] * 9,
        out_specs=[any_] * 3 + [vmem] * 13,
        scratch_shapes=[
            pltpu.VMEM((3, 4, width, width), low),
            pltpu.VMEM((2, 4 * PAD, width), low),
            pltpu.VMEM((CHIPS * 8, side), wide),
            pltpu.VMEM((CHIPS * 8, BAND), wide),
            pltpu.VMEM((CHIPS * 8, BAND), wide),
            pltpu.VMEM((4, 8, BAND), wide),
            pltpu.VMEM((4, 8, BAND), wide),
            pltpu.VMEM((4, 8, BAND), wide),
            pltpu.VMEM((3, 8, BAND), wide),
            pltpu.VMEM((2, 8, BAND), wide),
            pltpu.VMEM((2, 8, count), jnp.int32),
            pltpu.VMEM((count, 2 * count), wide),
            pltpu.VMEM((count, width), wide),
            pltpu.VMEM((4, count, width), low),
            pltpu.VMEM((count, width), low),
            pltpu.VMEM((2, count, width), wide),
            dma((2, 3)), dma((2, 3)), dma((3, 3)), dma((3, 3)),
            dma((3, 4, 2)), dma((3, 4, 2)), dma((3, 4, 2)), dma((3, 4, 2)),
            dma((3, 4)), dma((3, 4)), dma((3, 4)), dma((3, 4)),
            dma((3, 4, 4)), dma((3, 4, 4)),
            dma((CHIPS - 1,)), dma((CHIPS - 1,)), dma, dma, dma((4,)), dma((4,)),
            dma((4,)), dma((4,)), dma((4,)), dma((4,)), dma((3,)), dma((3,)), dma, dma, dma, dma,
            dma((2,)), dma((2,)), dma((3,)), dma((4,)), dma((2,)),
        ],
        compiler_params=pltpu.CompilerParams(
            collective_id=0, has_side_effects=True, vmem_limit_bytes=63 * 2**20
        ),
        name="forward",
    )(shards, down, acts, ada, tokens, cot, seg_col, seg_row, bins)
def slot_of(kind, zy, group):
    return zy * 4 + group if kind == 2 else group * 8 + zy


def add_rows(dst, sources, start, rows):
    def body(i, carry):
        where = pl.ds(pl.multiple_of(start + i * 16, 16), 16)
        total = dst[where, :].astype(jnp.float32)
        for source in sources:
            total = total + source[where, :].astype(jnp.float32)
        dst[where, :] = total.astype(dst.dtype)
        return carry

    lax.fori_loop(0, rows // 16, body, 0)


def scatter_kernel(share, g1_ref, g2_ref, g3_ref, rows_ref, down_ref, held, from_core, diag,
                   from_x, from_y, from_z, spare, *sems):
    (
        load_sem, c_send, c_recv, dx_send, dx_recv, dy_send, dy_recv, x_send, x_recv,
        y_send, y_recv, z_send, z_recv, group_send, group_recv,
    ) = sems
    z, y, x, c = position()
    group = x * 2 + c
    rows = 4 * share
    x_peer, y_peer, c_peer = device(z, y, 1 - x, c), device(z, 1 - y, x, c), device(z, y, x, 1 - c)
    halves = (pl.ds(0, CUT), pl.ds(CUT, rows - CUT))
    given = (g1_ref, g2_ref, g3_ref)
    greet(
        [device((z + k) % 4, y, x, c) for k in (1, 2, 3)]
        + [x_peer, y_peer, c_peer, device(z, y, 1 - x, 1 - c)]
    )
    sends = []

    def send(*args):
        copy = remote(*args)
        copy.start()
        sends.append(copy)

    places = ((0, 0), (0, 1), (1, 0), (1, 1))
    loads = {}

    def begin(a, k):
        zz = (z + k) % 4
        for pos, (oy, ox) in enumerate(places):
            yy = 1 - y if oy else y
            xx = 1 - x if ox else x
            send(
                given[a].at[slot_of(a, zz * 2 + yy, xx * 2 + 1 - c)],
                from_core.at[a, k, pos],
                c_send.at[a, k, pos],
                c_recv.at[a, k, pos],
                c_peer,
            )
            loads[a, k, pos] = pltpu.make_async_copy(
                given[a].at[slot_of(a, zz * 2 + yy, xx * 2 + c)],
                held.at[a, k, pos],
                load_sem.at[a, k, pos],
            )
            loads[a, k, pos].start()

    def pair(a, k):
        for pos in (3, 1, 2, 0):
            loads[a, k, pos].wait()
            arrive(from_core.at[a, k, pos], c_recv.at[a, k, pos], c_peer)
            add_rows(held.at[a, k, pos], [from_core.at[a, k, pos]], 0, rows)
            if pos == 3:
                top, low = held.at[a, k, 3, halves[0]], held.at[a, k, 3, halves[1]]
                send(top, diag.at[a, k, halves[0]], dy_send.at[a, k], dy_recv.at[a, k], y_peer)
                send(low, diag.at[a, k, halves[1]], dx_send.at[a, k], dx_recv.at[a, k], x_peer)
            if pos == 1:
                send(held.at[a, k, 1, halves[1]], from_x.at[a, k, halves[1]], x_send.at[a, k, 1], x_recv.at[a, k, 1], x_peer)
            if pos == 2:
                send(held.at[a, k, 2, halves[0]], from_y.at[a, k, halves[0]], y_send.at[a, k, 0], y_recv.at[a, k, 0], y_peer)

    def relay(a, k):
        arrive(diag.at[a, k, halves[0]], dy_recv.at[a, k], y_peer)
        add_rows(held.at[a, k, 1], [diag.at[a, k]], 0, CUT)
        send(held.at[a, k, 1, halves[0]], from_x.at[a, k, halves[0]], x_send.at[a, k, 0], x_recv.at[a, k, 0], x_peer)
        arrive(diag.at[a, k, halves[1]], dx_recv.at[a, k], x_peer)
        add_rows(held.at[a, k, 2], [diag.at[a, k]], CUT, rows - CUT)
        send(held.at[a, k, 2, halves[1]], from_y.at[a, k, halves[1]], y_send.at[a, k, 1], y_recv.at[a, k, 1], y_peer)

    def plane(a, k):
        for h in (0, 1):
            arrive(from_x.at[a, k, halves[h]], x_recv.at[a, k, h], x_peer)
            arrive(from_y.at[a, k, halves[h]], y_recv.at[a, k, h], y_peer)
        if k:
            add_rows(held.at[a, k, 0], [from_x.at[a, k], from_y.at[a, k]], 0, rows)
            send(held.at[a, k, 0], from_z.at[a, k - 1], z_send.at[a, k - 1], z_recv.at[a, k - 1], device((z + k) % 4, y, x, c))
            return
        for j in (1, 2, 3):
            arrive(from_z.at[a, j - 1], z_recv.at[a, j - 1], device((z - j + 4) % 4, y, x, c))

        def body(i, carry):
            where = pl.ds(pl.multiple_of(i * 16, 16), 16)
            total = held[a, 0, 0, where, :].astype(jnp.float32)
            total = total + from_x[a, 0, where, :].astype(jnp.float32)
            total = total + from_y[a, 0, where, :].astype(jnp.float32)
            for j in range(3):
                total = total + from_z[a, j, where, :].astype(jnp.float32)
            if a == 2:
                down_ref[where, :] = total
            else:
                held[a, 0, 0, where, :] = total.astype(jnp.bfloat16)
            return carry

        lax.fori_loop(0, rows // 16, body, 0)
        if a == 2:
            return
        picked = row_selector(rows, share)
        spare[a] = lax.dot_general(
            picked, held[a, 0, 0], (((0,), (0,)), ((), ())), preferred_element_type=jnp.float32
        ).astype(jnp.bfloat16)
        for j, (px, pc) in enumerate(partners):
            send(
                spare.at[a, pl.ds(pl.multiple_of((px * 2 + pc) * PAD, 16), PAD)],
                rows_ref.at[a, group],
                group_send.at[a, j],
                group_recv.at[a, j],
                device(z, y, px, pc),
            )
        rows_ref[a, group] = spare[a, pl.ds(pl.multiple_of(group * PAD, 16), PAD), :]

    partners = [(x, 1 - c), (1 - x, c), (1 - x, 1 - c)]
    order = [(a, k) for a in (2, 1, 0) for k in (1, 2, 3, 0)]
    for i in range(3):
        begin(*order[i])
    for i in range(len(order) + 2):
        if i + 3 < len(order):
            begin(*order[i + 3])
        if i < len(order):
            pair(*order[i])
        if 1 <= i < len(order) + 1:
            relay(*order[i - 1])
        if 2 <= i:
            plane(*order[i - 2])
    for a in range(2):
        for j, (px, pc) in enumerate(partners):
            arrive(rows_ref.at[a, px * 2 + pc], group_recv.at[a, j], device(z, y, px, pc))
    for copy in sends:
        copy.wait_send()


def scatter_grads(first, second, third, share):
    rows, width = third.shape[-2:]
    dma = pltpu.SemaphoreType.DMA
    low = jnp.bfloat16
    return pl.pallas_call(
        partial(scatter_kernel, share),
        out_shape=(
            jax.ShapeDtypeStruct((2, 4, PAD, width), low),
            jax.ShapeDtypeStruct((rows, width), jnp.float32),
        ),
        in_specs=[pl.BlockSpec(memory_space=pl.ANY)] * 3,
        out_specs=[pl.BlockSpec(memory_space=pltpu.VMEM)] * 2,
        scratch_shapes=[
            pltpu.VMEM((3, 4, 4, rows, width), low),
            pltpu.VMEM((3, 4, 4, rows, width), low),
            pltpu.VMEM((3, 4, rows, width), low),
            pltpu.VMEM((3, 4, rows, width), low),
            pltpu.VMEM((3, 4, rows, width), low),
            pltpu.VMEM((3, 3, rows, width), low),
            pltpu.VMEM((2, 4 * PAD, width), low),
            dma((3, 4, 4)), dma((3, 4, 4)), dma((3, 4, 4)),
            dma((3, 4)), dma((3, 4)), dma((3, 4)), dma((3, 4)),
            dma((3, 4, 2)), dma((3, 4, 2)), dma((3, 4, 2)), dma((3, 4, 2)),
            dma((3, 3)), dma((3, 3)), dma((2, 3)), dma((2, 3)),
        ],
        compiler_params=pltpu.CompilerParams(
            collective_id=1, has_side_effects=True, vmem_limit_bytes=58 * 2**20
        ),
        name="scatter_grads",
    )(first, second, third)


def layer_norm(values):
    center = values - jnp.mean(values, axis=-1, keepdims=True)
    inverse = lax.rsqrt(jnp.mean(center * center, axis=-1, keepdims=True) + EPSILON)
    return (center * inverse, inverse)


def norm_back(grad_normed, normed, inverse):
    return inverse * (
        grad_normed
        - jnp.mean(grad_normed, axis=-1, keepdims=True)
        - normed * jnp.mean(grad_normed * normed, axis=-1, keepdims=True)
    )


def to_heads(array):
    return array.reshape(array.shape[0], HEADS, array.shape[1] // HEADS)


def dots(spec, left, right):
    return jnp.einsum(spec, left, right, preferred_element_type=jnp.float32)


def masked_scores(query_heads, key_heads, same_crop):
    scale_factor = 1.0 / math.sqrt(query_heads.shape[-1])
    scores = dots("qhd,khd->hqk", query_heads, key_heads) * scale_factor
    return jnp.where(same_crop[None], scores, LARGE_NEGATIVE)


def attend(query_seq, key_seq, value_seq, same_crop):
    scores = masked_scores(to_heads(query_seq), to_heads(key_seq), same_crop)
    row_max = jnp.max(scores, axis=-1, keepdims=True)
    raised = jnp.exp(scores - row_max)
    row_total = jnp.sum(raised, axis=-1, keepdims=True)
    probability = (raised / row_total).astype(jnp.bfloat16)
    context = dots("hqk,khd->qhd", probability, to_heads(value_seq))
    return (context.reshape(query_seq.shape[0], -1), (row_max + jnp.log(row_total))[..., 0])


def attend_back(query_seq, key_seq, value_seq, same_crop, log_total, grad_seq):
    query_heads = to_heads(query_seq)
    key_heads = to_heads(key_seq)
    value_heads = to_heads(value_seq)
    grad_heads = to_heads(grad_seq)
    scale_factor = 1.0 / math.sqrt(query_heads.shape[-1])
    scores = masked_scores(query_heads, key_heads, same_crop)
    probability = jnp.exp(scores - log_total[..., None])
    grad_prob = dots("qhd,khd->hqk", grad_heads, value_heads)
    inner = jnp.sum(probability * grad_prob, axis=-1, keepdims=True)
    grad_scores = (probability * (grad_prob - inner)).astype(jnp.bfloat16)
    grad_query = dots("hqk,khd->qhd", grad_scores, key_heads) * scale_factor
    grad_key = dots("hqk,qhd->khd", grad_scores, query_heads) * scale_factor
    grad_value = dots("hqk,qhd->khd", probability.astype(jnp.bfloat16), grad_heads)
    rows_here = query_seq.shape[0]
    rows_whole = key_seq.shape[0]
    return (
        grad_query.reshape(rows_here, -1),
        grad_key.reshape(rows_whole, -1),
        grad_value.reshape(rows_whole, -1),
    )


def kernel_inputs(segments, conditions, noise_bins, bin_counts, ada_weight, first, up_weight):
    share, width = first.shape[0], first.shape[1] // 4
    cores = lax.axis_size("sp")
    shards = jnp.stack([first, up_weight]).reshape(2, share, 4, width)
    shards = jnp.pad(shards.transpose(0, 2, 1, 3), ((0, 0), (0, 0), (0, PAD - share), (0, 0)))
    acts = jax.nn.silu(conditions.astype(jnp.float32)).astype(jnp.bfloat16)
    acts = acts.reshape(CROPS, CHIPS, cores, share)
    acts = lax.dynamic_index_in_dim(acts, lax.axis_index("sp"), 2, keepdims=False)
    acts = jnp.pad(acts.transpose(1, 0, 2), ((0, 0), (0, 0), (0, 128 - share)))
    counts = jnp.pad(bin_counts.astype(jnp.bfloat16), (0, 128 - NBINS))
    counts = jnp.broadcast_to(counts, (CHIPS, 1, 128))
    acts = jnp.pad(jnp.concatenate([acts, counts], axis=1), ((0, 0), (0, 11), (0, 0)))
    ada = jnp.pad(ada_weight, ((0, 128 - share), (0, 0)))
    count = segments.shape[0]
    seg_col = jnp.broadcast_to(segments[:, None], (count, 128))
    seg_row = jnp.broadcast_to(segments[None, :], (8, count))
    bins = jnp.pad(noise_bins, (0, 4), constant_values=-1)
    bins = (bins[:, None] == jnp.arange(128, dtype=jnp.int32)).astype(jnp.float32)
    return shards, acts, ada, seg_col, seg_row, bins


def forward_plain(tokens_float, segments, conditions, noise_bins, bin_counts, ada_weight, first, up_weight,
                  down_weight):
    groups, cores = lax.axis_size("dp"), lax.axis_size("sp")
    share, width = first.shape[0], tokens_float.shape[1]
    index = lax.axis_index("dp") * cores + lax.axis_index("sp")
    mixers = lax.all_gather(first, ("dp", "sp"), axis=0, tiled=True)
    uppers = lax.all_gather(up_weight, ("dp", "sp"), axis=0, tiled=True)
    downers = lax.all_gather(down_weight, ("dp", "sp"), axis=0, tiled=True)
    mixers = mixers.reshape(width, 4, width).transpose(1, 0, 2)
    uppers = uppers.reshape(width, 4, width).transpose(1, 0, 2)
    downers = downers.reshape(4, width, width)
    bin_total = lax.psum(bin_counts, "dp")
    bin_weight = 40.0 * groups / bin_total.astype(jnp.float32)
    crop_weight = jnp.sum(
        jnp.where(noise_bins[:, None] == jnp.arange(NBINS, dtype=jnp.int32), bin_weight, 0.0),
        axis=-1,
    )
    cond_all = lax.all_gather(conditions, "dp", axis=0, tiled=True)
    cond_here = lax.dynamic_slice_in_dim(cond_all, index * share, share, axis=1)
    cond_act = jax.nn.silu(cond_here.astype(jnp.float32)).astype(jnp.bfloat16)
    modulation_part = dots("sd,df->sf", cond_act, ada_weight).reshape(groups, CROPS, -1)
    modulation = lax.psum(lax.psum_scatter(modulation_part, "dp", scatter_dimension=0), "sp")
    selector = (segments[:, None] == jnp.arange(CROPS, dtype=jnp.int32)).astype(jnp.float32)
    per_token = jnp.einsum("tc,cf->tf", selector, modulation, precision=lax.Precision.HIGHEST)
    shift_one, scale_one, gate_one, shift_two, scale_two, _ = jnp.split(per_token, 6, axis=-1)
    normed_one, _ = layer_norm(tokens_float)
    hidden_one = (normed_one * (1.0 + scale_one) + shift_one).astype(jnp.bfloat16)
    projected = dots("td,qdf->qtf", hidden_one, mixers[:3]).astype(jnp.bfloat16)
    sides = lax.all_gather(projected[1:], "sp", axis=1, tiled=True)
    all_segments = lax.all_gather(segments, "sp", axis=0, tiled=True)
    same_crop = segments[:, None] == all_segments[None, :]
    context, log_total = attend(projected[0], sides[0], sides[1], same_crop)
    context_low = context.astype(jnp.bfloat16)
    attended = dots("td,df->tf", context_low, mixers[3])
    middle = tokens_float + gate_one * attended
    normed_two, _ = layer_norm(middle)
    hidden_two = (normed_two * (1.0 + scale_two) + shift_two).astype(jnp.bfloat16)
    upper_in = dots("td,qdf->qtf", hidden_two, uppers)
    activated = jax.nn.gelu(upper_in, approximate=True).astype(jnp.bfloat16)
    slope = jax.vjp(partial(jax.nn.gelu, approximate=True), upper_in)[1](jnp.ones_like(upper_in))[0]
    mlp_out = dots("qtf,qfd->td", activated, downers)
    return (
        (mixers, uppers, downers), activated, slope, hidden_one, projected[0], sides, log_total,
        context_low, attended, middle, hidden_two, mlp_out, modulation, cond_act, crop_weight, same_crop,
    )


def on_device(
    chips,
    tokens_in,
    segment_ids,
    conditions,
    noise_bins,
    bin_counts,
    cotangent,
    ada_weight,
    qkv_weight,
    out_weight,
    up_weight,
    down_weight,
):
    tokens_float = tokens_in[0].astype(jnp.float32)
    segments = segment_ids[0]
    width = tokens_float.shape[1]
    share = qkv_weight.shape[0]
    kernels = chips and 4 * share == down_weight.shape[0]
    first = jnp.concatenate([qkv_weight, out_weight], axis=1)
    if kernels:
        shards, acts, ada, seg_col, seg_row, bins = kernel_inputs(
            segments, conditions[0], noise_bins[0], bin_counts[0], ada_weight, first, up_weight
        )
        (
            weights, down_part, slope, hidden_one, queries, sides, log_total, context_low, attended,
            middle, hidden_two, mlp_out, tokens_out, table, conds, level,
        ) = run_forward(
            shards, down_weight, acts, ada, tokens_in[0], cotangent[0], seg_col, seg_row, bins, share
        )
        mixers, uppers, downers = weights[0], weights[1], weights[2]
        modulation = jnp.concatenate([table[:CROPS], table[CROPS:]], axis=1)
        cond_act = conds[:, :CROPS, :share].reshape(-1, share)
        crop_weight = level[:CROPS, 0]
        log_total = log_total[:, :HEADS].T
        all_segments = lax.all_gather(segments, "sp", axis=0, tiled=True)
        same_crop = segments[:, None] == all_segments[None, :]
    else:
        (
            (mixers, uppers, downers), activated, slope, hidden_one, queries, sides, log_total,
            context_low, attended, middle, hidden_two, mlp_out, modulation, cond_act, crop_weight, same_crop,
        ) = forward_plain(
            tokens_float, segments, conditions[0], noise_bins[0], bin_counts[0], ada_weight, first,
            up_weight, down_weight,
        )
    selector = (segments[:, None] == jnp.arange(CROPS, dtype=jnp.int32)).astype(jnp.float32)
    per_token = jnp.einsum("tc,cf->tf", selector, modulation, precision=lax.Precision.HIGHEST)
    _, scale_one, gate_one, _, scale_two, gate_two = jnp.split(per_token, 6, axis=-1)
    normed_one, inverse_one = layer_norm(tokens_float)
    normed_two, inverse_two = layer_norm(middle)

    token_weight = jnp.sum(selector * crop_weight[None, :], axis=-1)
    grad_out = cotangent[0].astype(jnp.float32) * token_weight[:, None]
    grad_mlp = (grad_out * gate_two).astype(jnp.bfloat16)
    if not kernels:
        tokens_out = (middle + gate_two * mlp_out).astype(jnp.bfloat16)
        down_part = dots("qtf,td->qfd", activated, grad_mlp).astype(jnp.bfloat16)
    grad_act = dots("td,qfd->qtf", grad_mlp, downers)
    grad_upper = (grad_act * slope).astype(jnp.bfloat16)
    up_part = dots("td,qtf->qdf", hidden_two, grad_upper).astype(jnp.bfloat16)
    grad_hidden_two = dots("qtf,qdf->td", grad_upper, uppers)
    grad_middle = grad_out + norm_back(grad_hidden_two * (1.0 + scale_two), normed_two, inverse_two)
    grad_attended = (grad_middle * gate_one).astype(jnp.bfloat16)
    grad_context = dots("tf,df->td", grad_attended, mixers[3]).astype(jnp.bfloat16)
    grad_query, grad_key, grad_value = attend_back(
        queries, sides[0], sides[1], same_crop, log_total, grad_context
    )
    grad_sides = lax.psum_scatter(
        jnp.stack([grad_key, grad_value]).astype(jnp.bfloat16),
        "sp",
        scatter_dimension=1,
        tiled=True,
    )
    grad_projected = jnp.concatenate([grad_query.astype(jnp.bfloat16)[None], grad_sides])
    out_part = dots("td,tf->df", context_low, grad_attended).astype(jnp.bfloat16)
    qkv_part = dots("td,qtf->qdf", hidden_one, grad_projected).astype(jnp.bfloat16)
    first_part = jnp.concatenate([qkv_part, out_part[None]])
    grad_hidden_one = dots("qtf,qdf->td", grad_projected, mixers[:3])
    tokens_grad = grad_middle + norm_back(
        grad_hidden_one * (1.0 + scale_one), normed_one, inverse_one
    )

    if kernels:
        pieces = (32, 4 * share, width)
        rows, down_grad = scatter_grads(
            first_part.reshape(pieces), up_part.reshape(pieces), down_part.reshape(pieces), share
        )
        rows = rows[:, :, :share].astype(jnp.float32).transpose(0, 2, 1, 3).reshape(2, share, 4 * width)
        first_grad, up_grad = rows[0], rows[1]
    else:
        joined = jnp.stack([first_part, up_part]).transpose(2, 0, 1, 3).reshape(width, 8 * width)
        rows = lax.psum_scatter(joined, ("dp", "sp"), scatter_dimension=0, tiled=True)
        rows = rows.astype(jnp.float32)
        first_grad, up_grad = rows[:, : 4 * width], rows[:, 4 * width :]
        down_grad = lax.psum_scatter(
            down_part.reshape(4 * width, width), ("dp", "sp"), scatter_dimension=0, tiled=True
        ).astype(jnp.float32)

    grad_per_token = jnp.concatenate(
        [
            grad_hidden_one,
            grad_hidden_one * normed_one,
            grad_middle * attended,
            grad_hidden_two,
            grad_hidden_two * normed_two,
            grad_out * mlp_out,
        ],
        axis=-1,
    )
    grad_modulation = lax.psum(
        jnp.einsum("tc,tf->cf", selector, grad_per_token, precision=lax.Precision.HIGHEST), "sp"
    )
    grad_rows = lax.all_gather(grad_modulation, "dp", axis=0, tiled=True)
    ada_grad = jnp.einsum(
        "sd,sf->df", cond_act.astype(jnp.float32), grad_rows, precision=lax.Precision.HIGHEST
    )
    silu_part = jnp.einsum(
        "sf,df->sd", grad_rows, ada_weight.astype(jnp.float32), precision=lax.Precision.HIGHEST
    )
    silu_all = lax.all_gather(silu_part, ("dp", "sp"), axis=0)
    silu_here = lax.dynamic_slice_in_dim(silu_all, lax.axis_index("dp") * CROPS, CROPS, axis=1)
    grad_silu = silu_here.transpose(1, 0, 2).reshape(CROPS, width)
    silu_pull = jax.vjp(jax.nn.silu, conditions[0].astype(jnp.float32))[1]
    cond_grad = silu_pull(grad_silu)[0]
    return (
        tokens_out[None],
        tokens_grad[None],
        cond_grad[None],
        ada_grad,
        first_grad[:, : 3 * width],
        first_grad[:, 3 * width :],
        up_grad,
        down_grad,
    )


def solution(mesh):
    placed = (
        P("dp", "sp", None),
        P("dp", "sp"),
        P("dp", None, None),
        P("dp", None),
        P("dp", None),
        P("dp", "sp", None),
        P(("dp", "sp"), None),
        P(("dp", "sp"), None),
        P(("dp", "sp"), None),
        P(("dp", "sp"), None),
        P(("dp", "sp"), None),
    )
    return jax.shard_map(
        partial(on_device, mesh.shape["dp"] == 16 and mesh.shape["sp"] == 2),
        mesh=mesh,
        in_specs=placed,
        out_specs=(
            P("dp", "sp", None),
            P("dp", "sp", None),
            P("dp", None, None),
            P(("dp", "sp"), None),
            P(("dp", "sp"), None),
            P(("dp", "sp"), None),
            P(("dp", "sp"), None),
            P(("dp", "sp"), None),
        ),
        check_vma=False,
    )
```

profile of v0, /device:TPU:0, one launch (start us, length us, event | category | flops | bytes accessed | tf_op | source)
XLA Modules:
  0.0 567.2 jit_solution(18174865870780788353)
XLA Ops:
  17.5 185.3 %forward.1 = (bf16[3,4,1152,1152]{3,2,1,0:T(8,128)(2,1)}, bf16[4,1152,1152]{2,1,0:T(8,128)(2,1)}, f32[4,256,1152]{2,1,0:T(8,128)}, bf16[256,1152]{1,0:T(8,128)(2...) custom-call(bf16[2,4,48,1152]{3,2,1,0:T(8,128)(2,1)} %pad.24.shards_, ...), custom_call_target="tpu_custom_call" | custom-call | tf_op jit(solution)/shard_map/forward/pallas_call | solution.py:464
  206.4 3.0 fusion.58
  209.4 11.2 %fusion.11 = bf16[4,256,1152]{2,1,0:T(8,128)(2,1)S(1)} fusion(f32[4,256,1152]{2,1,0:T(8,128)} %get-tuple-element.31, bf16[3,4,1152,1152]{3,2,1,0:T(8,128)(2,1)} %get-tuple-element.29, f32[256,6912]{1,0:T(8,128)S(1)} %fusion.58, f32[256]{0:T(256)S(1)} %select_reduce_fusion, bf16[1,256,1152]{2,1,0:T(8,128)(2,1)S(1)} %copy-done.8), kind=kOutput, calls=%fused_computation.19 | convolution fusion | flops 2721447936 | bytes 19465216 | tf_op jit(solution)/shard_map/td,qfd->qtf/dot_general | solution.py:711
  220.7 8.3 %fusion.76 = (f32[256]{0:T(256)S(1)}, f32[256]{0:T(256)S(1)}, f32[256,1152]{1,0:T(8,128)S(1)}) fusion(f32[256,6912]{1,0:T(8,128)S(1)} %fusion.58, f32[256]{0:T(256)S(1)} %add_rsqrt_fusion.1, f32[256,1152]{1,0:T(8,128)S(1)} %copy-done.1, f32[256]{0:T(256)S(1)} %broadcast_multiply_fusion.5, bf16[4,256,1152]{2,1,0:T(8,128)(2,1)S(1)} %fusion.11, ...), kind=kOutput, calls=%fused_computation.119 | convolution fusion | flops 2719972864 | bytes 16519168 | tf_op jit(solution)/shard_map/qtf,qdf->td/dot_general | solution.py:711
  231.5 2.8 fusion.30
  235.4 3.2 fusion.78
  244.8 2.6 copy.118
  248.3 2.5 fusion.81
  250.8 3.4 fusion.33
  254.2 3.6 multiply_reduce_fusion
  257.8 2.4 multiply_convert_fusion
  260.2 2.4 multiply_convert_fusion.1
  262.6 2.4 copy.119
  267.4 3.3 pad_maximum_fusion.1
  271.1 4.4 fusion.41
  280.9 8.6 %convolution_convert_fusion = bf16[4,1152,1152]{1,2,0:T(8,128)(2,1)} fusion(bf16[4,256,1152]{2,1,0:T(8,128)(2,1)} %copy-done.6, bf16[256,1152]{1,0:T(8,128)(2,1)S(1)} %copy-done.20), kind=kOutput, calls=%fused_computation | convolution fusion | flops 2723217408 | bytes 13565952 | tf_op jit(solution)/shard_map/td,qtf->qdf/dot_general | solution.py:711
  289.6 7.1 %fusion.77 = (f32[256]{0:T(256)S(1)}, f32[256]{0:T(256)S(1)}, f32[256,6912]{1,0:T(8,128)S(1)}, f32[256,1152]{1,0:T(8,128)S(1)}) fusion(f32[256,6912]{1,0:T(8,128)} %copy-done.2, f32[256]{0:T(256)} %add_rsqrt_fusion, f32[256]{0:T(256)} %copy-done.31, bf16[1,256,1152]{2,1,0:T(8,128)(2,1)} %param.11, bf16[3,4,1152,1152]{3,2,1,0:T(8,128)(2,1)} %get-tuple-element.29, ...), kind=kOutput, calls=%fused_computation.120 | convolution fusion | flops 2041675264 | bytes 13864960 | tf_op jit(solution)/shard_map/qtf,qdf->td/dot_general | solution.py:711
  296.7 2.9 fusion.47
  302.1 3.0 fusion.66
  307.7 22.6 %all-reduce.8.cloned.1.call-done = f32[4,6912]{1,0:T(4,128)} async-done(((f32[4,6912]{1,0:T(4,128)}), f32[4,6912]{1,0:T(4,128)}) %all-reduce.8.cloned.1.call-update) | async-done | bytes 110608 | tf_op jit(solution)/shard_map/psum | solution.py:930
  330.3 3.8 fusion
  334.1 4.8 pad_maximum_fusion
  338.9 170.5 %scatter_grads.1 = (bf16[2,4,48,1152]{3,2,1,0:T(8,128)(2,1)}, f32[144,1152]{1,0:T(8,128)}) custom-call(bf16[32,144,1152]{2,1,0:T(8,128)(2,1)} %bitcast.134, bf16[32,144,1152]{2,1,0:T(8,128)(2,1)} %bitcast.133, bf16[32,144,1152]{2,1,0:T(8,128)(2,1)} %bitcast.137), custom_call_target="tpu_custom_call" | custom-call | tf_op jit(solution)/shard_map/scatter_grads/pallas_call | solution.py:664
  518.7 38.8 %all-gather.3 = f32[32,64,36]{1,2,0:T(8,128)S(1)} all-gather(f32[1,64,36]{1,2,0:T(8,128)S(1)} %convolution_bitcast_fusion), channel_id=3, replica_groups=mesh['dp'=16,'sp'=2] {'dp','sp'}, dimensions={0}, use_global_device_ids=true | all-gather | bytes 304128 | tf_op jit(solution)/shard_map/all_gather | solution.py:940
  (148 shorter events, 49.7 us)
Async XLA Ops:
  7.2 3.6 copy-start.21
  7.2 282.4 %reduce-scatter.2.cloned.1.call-start = ((), (), s32[]{:S(2)}) async-start(), calls=%async_computation.1 | async-start | bytes 3538944 | tf_op jit(solution)/shard_map/reduce_scatter | solution.py:888
  11.1 3.0 copy-start.22
  202.7 3.4 copy-start.1
  204.7 24.4 %copy-start.27 = (f32[256]{0:T(256)}, f32[256]{0:T(256)S(1)}, u32[]{:S(2)}) copy-start(f32[256]{0:T(256)S(1)} %select_reduce_fusion) | copy-start | bytes 3076
  206.1 22.9 %copy-start.25 = (f32[256]{0:T(256)}, f32[256]{0:T(256)S(1)}, u32[]{:S(2)}) copy-start(f32[256]{0:T(256)S(1)} %broadcast_multiply_fusion.5) | copy-start | bytes 3076
  206.4 22.7 %copy-start.29 = (f32[256]{0:T(256)}, f32[256]{0:T(256)S(1)}, u32[]{:S(2)}) copy-start(f32[256]{0:T(256)S(1)} %add_rsqrt_fusion.1) | copy-start | bytes 3076
  206.4 3.0 copy-start.8
  209.4 19.7 %copy-start.2 = (f32[256,6912]{1,0:T(8,128)}, f32[256,6912]{1,0:T(8,128)S(1)}, u32[]{:S(2)}) copy-start(f32[256,6912]{1,0:T(8,128)S(1)} %fusion.58) | copy-start | bytes 21233668
  220.7 8.4 %copy-start.6 = (bf16[4,256,1152]{2,1,0:T(8,128)(2,1)}, bf16[4,256,1152]{2,1,0:T(8,128)(2,1)S(1)}, u32[]{:S(2)}) copy-start(bf16[4,256,1152]{2,1,0:T(8,128)(2,1)S(1)} %fusion.11) | copy-start | bytes 7077892
  248.3 2.5 copy-start.12
  250.8 3.4 copy-start.10
  270.7 59.6 %all-reduce.8.cloned.1.call-start = ((), (), s32[]{:S(2)}) async-start(), calls=%async_computation.2 | async-start | bytes 221184 | tf_op jit(solution)/shard_map/psum | solution.py:930
  275.5 4.2 copy-start.4
  275.5 5.4 copy-start.20
  289.5 7.1 %copy-start.3 = (f32[256,1152]{1,0:T(8,128)S(1)}, f32[256,1152]{1,0:T(8,128)}, u32[]{:S(2)}) copy-start(f32[256,1152]{1,0:T(8,128)} %get-tuple-element.49) | copy-start | bytes 3538948
  289.6 7.1 %copy-start.5 = (bf16[1,256,1152]{2,1,0:T(8,128)(2,1)S(1)}, bf16[1,256,1152]{2,1,0:T(8,128)(2,1)}, u32[]{:S(2)}) copy-start(bf16[1,256,1152]{2,1,0:T(8,128)(2,1)} %param.11) | copy-start | bytes 1769476
  289.6 7.1 %copy-start.32 = (f32[256]{0:T(256)S(1)}, f32[256]{0:T(256)}, u32[]{:S(2)}) copy-start(f32[256]{0:T(256)} %copy-done.31) | copy-start | bytes 3076
  289.6 7.2 %copy-start.33 = (f32[256]{0:T(256)S(1)}, f32[256]{0:T(256)}, u32[]{:S(2)}) copy-start(f32[256]{0:T(256)} %add_rsqrt_fusion) | copy-start | bytes 3076
  296.7 2.9 copy-start.15
  305.2 208.7 %all-gather.6.cloned.1.call-start = ((), (), s32[]{:S(2)}) async-start(), calls=%async_computation.3 | async-start | bytes 1880064 | tf_op jit(solution)/shard_map/all_gather | solution.py:933
  305.4 24.9 %copy-start.11 = (bf16[1,256,1152]{2,1,0:T(8,128)(2,1)S(1)}, bf16[1,256,1152]{2,1,0:T(8,128)(2,1)}, u32[]{:S(2)}) copy-start(bf16[1,256,1152]{2,1,0:T(8,128)(2,1)} %copy.121) | copy-start | bytes 1769476
  518.7 39.5 %copy-start.24 = (bf16[1,4,1152]{2,1,0:T(4,128)(2,1)S(1)}, bf16[1,4,1152]{2,1,0:T(4,128)(2,1)}, u32[]{:S(2)}) copy-start(bf16[1,4,1152]{2,1,0:T(4,128)(2,1)} %param.13) | copy-start | bytes 27652
  518.7 40.1 %copy-start.19 = (bf16[256,1152]{1,0:T(8,128)(2,1)S(1)}, bf16[256,1152]{1,0:T(8,128)(2,1)}, u32[]{:S(2)}) copy-start(bf16[256,1152]{1,0:T(8,128)(2,1)} %get-tuple-element.26) | copy-start | bytes 1769476
  (14 other events, 20.6 us)
Sparse Core Ops, SparseCore 0:
  270.8 16.8 reduce-scatter.1
  305.3 24.9 all-reduce.7
  333.4 74.1 all-gather.5
where the time goes:
time: 572 us; the launch traced here: 567 us
  Pallas kernels  356 us (62%)
  matrix products  69.1 us (12%)
  blocking collectives  40.8 us (7%)
  local copies, waits for them, and re-layouts  38.9 us (7%)
  other arithmetic  24.6 us (4%)
  waiting for transfers between devices  22.6 us (4%)
  between operations  14.6 us (3%)
    pallas_call x1, Pallas kernels, run_forward(): pl.pallas_call(partial(forward_kernel, share), out_shape=(out((3, 4, widt...  185 us
    pallas_call x1, Pallas kernels, scatter_grads(): pl.pallas_call(partial(scatter_kernel, share), out_shape=(jax.ShapeDtypeS...  171 us
    dot_general x12, matrix products, dots(): return jnp.einsum(spec, left, right, preferred_element_type=jnp.float32)  60.3 us
    all_gather x1, blocking collectives, on_device(): silu_all = lax.all_gather(silu_part, ('dp', 'sp'), axis=0)  38.8 us
    psum x1, waiting for transfers between devices, on_device(): lax.psum(jnp.einsum('tc,tf->cf', selector, grad_per_token, precision=lax....  22.6 us
  transfers between devices with their start and end apart: 3, of which 1 were waited for; matrix products, arithmetic and copies ran while one was open for 6% of the time, Pallas kernels for 30%

commit v1 on v0

--- a/solution.py
+++ b/solution.py
@@ -118,9 +118,9 @@
                    seg_row_ref, bins_ref,
                    weights_ref, down_part_ref, slope_ref, hidden_ref, query_ref, sides_ref, total_ref,
                    context_ref, attended_ref, middle_ref, hidden_two_ref, mlp_ref, out_ref, table_ref,
-                   conds_ref, level_ref,
+                   conds_ref, level_ref, grad_mlp, seg_all,
                    full, stage, part, part_recv, band, band_diag, band_x, band_y, band_z, halves_of,
-                   seg_all, bias, work, active, grad_mlp, slope, *sems):
+                   bias, work, active, slope, *sems):
     (
         group_send, group_recv, z_send, z_recv, x_send, x_recv, y_send, y_recv,
         dx_send, dx_recv, dy_send, dy_recv, c_send, c_recv,
@@ -480,9 +480,11 @@
             out((8, side), wide),
             out((CHIPS, 16, 128), low),
             out((8, 128), wide),
+            out((count, width), low),
+            out((2, 8, count), jnp.int32),
         ),
         in_specs=[vmem] * 9,
-        out_specs=[any_] * 3 + [vmem] * 13,
+        out_specs=[any_] * 3 + [vmem] * 15,
         scratch_shapes=[
             pltpu.VMEM((3, 4, width, width), low),
             pltpu.VMEM((2, 4 * PAD, width), low),
@@ -494,11 +496,9 @@
             pltpu.VMEM((4, 8, BAND), wide),
             pltpu.VMEM((3, 8, BAND), wide),
             pltpu.VMEM((2, 8, BAND), wide),
-            pltpu.VMEM((2, 8, count), jnp.int32),
             pltpu.VMEM((count, 2 * count), wide),
             pltpu.VMEM((count, width), wide),
             pltpu.VMEM((4, count, width), low),
-            pltpu.VMEM((count, width), low),
             pltpu.VMEM((2, count, width), wide),
             dma((2, 3)), dma((2, 3)), dma((3, 3)), dma((3, 3)),
             dma((3, 4, 2)), dma((3, 4, 2)), dma((3, 4, 2)), dma((3, 4, 2)),
@@ -513,8 +513,6 @@
         ),
         name="forward",
     )(shards, down, acts, ada, tokens, cot, seg_col, seg_row, bins)
-def slot_of(kind, zy, group):
-    return zy * 4 + group if kind == 2 else group * 8 + zy
 
 
 def add_rows(dst, sources, start, rows):
@@ -529,106 +527,125 @@
     lax.fori_loop(0, rows // 16, body, 0)
 
 
-def scatter_kernel(share, g1_ref, g2_ref, g3_ref, rows_ref, down_ref, held, from_core, diag,
-                   from_x, from_y, from_z, spare, *sems):
+def split_low(values):
+    high = values.astype(jnp.bfloat16)
+    return high, (values - high.astype(jnp.float32)).astype(jnp.bfloat16)
+
+
+def backward_kernel(share, weights_ref, down_part_ref, slope_ref, middle_ref, attended_ref, mlp_ref,
+                    hidden_ref, query_ref, sides_ref, total_ref, context_ref, hidden_two_ref,
+                    grad_mlp_ref, table_ref, conds_ref, level_ref, seg_all_ref, seg_col_ref, tokens_ref,
+                    cot_ref, ada_ref,
+                    mixer_part_ref, up_part_ref, rows_ref, down_ref, tokens_grad_ref, ada_grad_ref, silu_ref,
+                    held, from_core, diag, from_x, from_y, from_z, spare, block, part, quad, lows,
+                    work, grad_middle, grad_context, leave, enter, bias, sums, sums_row, sums_core, band, silu_part,
+                    *sems):
     (
         load_sem, c_send, c_recv, dx_send, dx_recv, dy_send, dy_recv, x_send, x_recv,
-        y_send, y_recv, z_send, z_recv, group_send, group_recv,
+        y_send, y_recv, z_send, z_recv, group_send, group_recv, block_sem, part_sem, quad_sem,
+        side_send, side_recv, m_send, m_recv, mz_send, mz_recv, mx_send, mx_recv, my_send, my_recv,
+        md_send, md_recv, mc_send, mc_recv, s_send, s_recv, sc_send, sc_recv,
     ) = sems
     z, y, x, c = position()
+    me = z * 4 + y * 2 + x
     group = x * 2 + c
     rows = 4 * share
+    count, width = tokens_ref.shape
+    halves = (pl.ds(0, CUT), pl.ds(CUT, rows - CUT))
     x_peer, y_peer, c_peer = device(z, y, 1 - x, c), device(z, 1 - y, x, c), device(z, y, x, 1 - c)
-    halves = (pl.ds(0, CUT), pl.ds(CUT, rows - CUT))
-    given = (g1_ref, g2_ref, g3_ref)
+    partners = [(x, 1 - c), (1 - x, c), (1 - x, 1 - c)]
     greet(
-        [device((z + k) % 4, y, x, c) for k in (1, 2, 3)]
-        + [x_peer, y_peer, c_peer, device(z, y, 1 - x, 1 - c)]
-    )
-    sends = []
-
-    def send(*args):
+        [((me + k) % CHIPS, c) for k in range(1, CHIPS)] + [c_peer, device(z, y, 1 - x, 1 - c)]
+    )
+    sends = {}
+
+    def send(owner, *args):
         copy = remote(*args)
         copy.start()
-        sends.append(copy)
-
-    places = ((0, 0), (0, 1), (1, 0), (1, 1))
+        sends.setdefault(owner, []).append(copy)
+
+    def finish_sends(owner):
+        for copy in sends.pop(owner, []):
+            copy.wait_send()
+
+    order = [(a, k) for a in (2, 1, 0) for k in (1, 2, 3, 0)]
+    given = (mixer_part_ref, up_part_ref, down_part_ref)
     loads = {}
 
-    def begin(a, k):
+    def begin(i):
+        a, k = order[i]
+        finish_sends(("held", i - 5))
         zz = (z + k) % 4
-        for pos, (oy, ox) in enumerate(places):
+        for pos, (oy, ox) in enumerate(PLACES):
             yy = 1 - y if oy else y
             xx = 1 - x if ox else x
-            send(
-                given[a].at[slot_of(a, zz * 2 + yy, xx * 2 + 1 - c)],
-                from_core.at[a, k, pos],
-                c_send.at[a, k, pos],
-                c_recv.at[a, k, pos],
-                c_peer,
-            )
-            loads[a, k, pos] = pltpu.make_async_copy(
-                given[a].at[slot_of(a, zz * 2 + yy, xx * 2 + c)],
-                held.at[a, k, pos],
-                load_sem.at[a, k, pos],
-            )
-            loads[a, k, pos].start()
-
-    def pair(a, k):
+            for core in (0, 1):
+                cc = 1 - c if core else c
+                where, row = block_of(a, zz * 2 + yy, xx * 2 + cc)
+                src = given[a].at[where, pl.ds(pl.multiple_of(row * rows, 16), rows)]
+                if core:
+                    send("core", src, from_core.at[i % 4, pos], c_send.at[i, pos], c_recv.at[i, pos], c_peer)
+                else:
+                    loads[i, pos] = pltpu.make_async_copy(src, held.at[i % 5, pos], load_sem.at[i, pos])
+                    loads[i, pos].start()
+
+    def pair(i):
         for pos in (3, 1, 2, 0):
-            loads[a, k, pos].wait()
-            arrive(from_core.at[a, k, pos], c_recv.at[a, k, pos], c_peer)
-            add_rows(held.at[a, k, pos], [from_core.at[a, k, pos]], 0, rows)
+            loads[i, pos].wait()
+            arrive(from_core.at[i % 4, pos], c_recv.at[i, pos], c_peer)
+            add_rows(held.at[i % 5, pos], [from_core.at[i % 4, pos]], 0, rows)
+            mine = held.at[i % 5, pos]
+            top, low = mine.at[halves[0]], mine.at[halves[1]]
             if pos == 3:
-                top, low = held.at[a, k, 3, halves[0]], held.at[a, k, 3, halves[1]]
-                send(top, diag.at[a, k, halves[0]], dy_send.at[a, k], dy_recv.at[a, k], y_peer)
-                send(low, diag.at[a, k, halves[1]], dx_send.at[a, k], dx_recv.at[a, k], x_peer)
+                send(("held", i), top, diag.at[i % 4, halves[0]], dy_send.at[i], dy_recv.at[i], y_peer)
+                send(("held", i), low, diag.at[i % 4, halves[1]], dx_send.at[i], dx_recv.at[i], x_peer)
             if pos == 1:
-                send(held.at[a, k, 1, halves[1]], from_x.at[a, k, halves[1]], x_send.at[a, k, 1], x_recv.at[a, k, 1], x_peer)
+                send(("held", i), low, from_x.at[i % 5, halves[1]], x_send.at[i, 1], x_recv.at[i, 1], x_peer)
             if pos == 2:
-                send(held.at[a, k, 2, halves[0]], from_y.at[a, k, halves[0]], y_send.at[a, k, 0], y_recv.at[a, k, 0], y_peer)
-
-    def relay(a, k):
-        arrive(diag.at[a, k, halves[0]], dy_recv.at[a, k], y_peer)
-        add_rows(held.at[a, k, 1], [diag.at[a, k]], 0, CUT)
-        send(held.at[a, k, 1, halves[0]], from_x.at[a, k, halves[0]], x_send.at[a, k, 0], x_recv.at[a, k, 0], x_peer)
-        arrive(diag.at[a, k, halves[1]], dx_recv.at[a, k], x_peer)
-        add_rows(held.at[a, k, 2], [diag.at[a, k]], CUT, rows - CUT)
-        send(held.at[a, k, 2, halves[1]], from_y.at[a, k, halves[1]], y_send.at[a, k, 1], y_recv.at[a, k, 1], y_peer)
-
-    def plane(a, k):
+                send(("held", i), top, from_y.at[i % 5, halves[0]], y_send.at[i, 0], y_recv.at[i, 0], y_peer)
+
+    def relay(i):
+        far = diag.at[i % 4]
+        arrive(far.at[halves[0]], dy_recv.at[i], y_peer)
+        add_rows(held.at[i % 5, 1], [far], 0, CUT)
+        top = held.at[i % 5, 1, halves[0]]
+        send(("held", i), top, from_x.at[i % 5, halves[0]], x_send.at[i, 0], x_recv.at[i, 0], x_peer)
+        arrive(far.at[halves[1]], dx_recv.at[i], x_peer)
+        add_rows(held.at[i % 5, 2], [far], CUT, rows - CUT)
+        low = held.at[i % 5, 2, halves[1]]
+        send(("held", i), low, from_y.at[i % 5, halves[1]], y_send.at[i, 1], y_recv.at[i, 1], y_peer)
+
+    def plane(i):
+        a, k = order[i]
         for h in (0, 1):
-            arrive(from_x.at[a, k, halves[h]], x_recv.at[a, k, h], x_peer)
-            arrive(from_y.at[a, k, halves[h]], y_recv.at[a, k, h], y_peer)
+            arrive(from_x.at[i % 5, halves[h]], x_recv.at[i, h], x_peer)
+            arrive(from_y.at[i % 5, halves[h]], y_recv.at[i, h], y_peer)
+        mine = held.at[i % 5, 0]
         if k:
-            add_rows(held.at[a, k, 0], [from_x.at[a, k], from_y.at[a, k]], 0, rows)
-            send(held.at[a, k, 0], from_z.at[a, k - 1], z_send.at[a, k - 1], z_recv.at[a, k - 1], device((z + k) % 4, y, x, c))
+            add_rows(mine, [from_x.at[i % 5], from_y.at[i % 5]], 0, rows)
+            send(("held", i), mine, from_z.at[a, k - 1], z_send.at[a, k - 1], z_recv.at[a, k - 1], device((z + k) % 4, y, x, c))
             return
         for j in (1, 2, 3):
             arrive(from_z.at[a, j - 1], z_recv.at[a, j - 1], device((z - j + 4) % 4, y, x, c))
 
-        def body(i, carry):
-            where = pl.ds(pl.multiple_of(i * 16, 16), 16)
-            total = held[a, 0, 0, where, :].astype(jnp.float32)
-            total = total + from_x[a, 0, where, :].astype(jnp.float32)
-            total = total + from_y[a, 0, where, :].astype(jnp.float32)
+        def body(at):
+            total = mine[at, :].astype(jnp.float32)
+            total = total + from_x[i % 5, at, :].astype(jnp.float32)
+            total = total + from_y[i % 5, at, :].astype(jnp.float32)
             for j in range(3):
-                total = total + from_z[a, j, where, :].astype(jnp.float32)
+                total = total + from_z[a, j, at, :].astype(jnp.float32)
             if a == 2:
-                down_ref[where, :] = total
+                down_ref[at, :] = total
             else:
-                held[a, 0, 0, where, :] = total.astype(jnp.bfloat16)
-            return carry
-
-        lax.fori_loop(0, rows // 16, body, 0)
+                mine[at, :] = total.astype(jnp.bfloat16)
+
+        chunks(rows, body)
         if a == 2:
             return
-        picked = row_selector(rows, share)
-        spare[a] = lax.dot_general(
-            picked, held[a, 0, 0], (((0,), (0,)), ((), ())), preferred_element_type=jnp.float32
-        ).astype(jnp.bfloat16)
+        spare[a] = product_by_rows(row_selector(rows, share), mine[...]).astype(jnp.bfloat16)
         for j, (px, pc) in enumerate(partners):
             send(
+                "end",
                 spare.at[a, pl.ds(pl.multiple_of((px * 2 + pc) * PAD, 16), PAD)],
                 rows_ref.at[a, group],
                 group_send.at[a, j],
@@ -637,56 +654,348 @@
             )
         rows_ref[a, group] = spare[a, pl.ds(pl.multiple_of(group * PAD, 16), PAD), :]
 
-    partners = [(x, 1 - c), (1 - x, c), (1 - x, 1 - c)]
-    order = [(a, k) for a in (2, 1, 0) for k in (1, 2, 3, 0)]
-    for i in range(3):
-        begin(*order[i])
+    uses = [(2, q) for q in range(4)] + [(1, q) for q in range(4)] + [(0, 3), (0, 0), (0, 1), (0, 2)]
+    coming = {}
+
+    def fetch(n):
+        if n < len(uses):
+            copy = pltpu.make_async_copy(weights_ref.at[uses[n]], block.at[n % 2], block_sem.at[n % 2])
+            copy.start()
+            coming[n] = copy
+
+    def take(n):
+        coming[n].wait()
+        return block[n % 2]
+
+    going = {}
+
+    def put(n, left, right, target):
+        if n - 2 in going:
+            going.pop(n - 2).wait()
+
+        def body(i, carry):
+            columns = pl.ds(pl.multiple_of(i * 384, 128), 384)
+            part[n % 2, columns, :] = product_by_rows(left[:, columns], right[...]).astype(jnp.bfloat16)
+            return carry
+
+        lax.fori_loop(0, width // 384, body, 0)
+        going[n] = pltpu.make_async_copy(part.at[n % 2], target, part_sem.at[n % 2])
+        going[n].start()
+
+    quads = {}
+
+    def slopes(q):
+        quads[q] = pltpu.make_async_copy(slope_ref.at[q], quad.at[q], quad_sem.at[q])
+        quads[q].start()
+
+    def through_down(q):
+        work[...] = product_by_columns(grad_mlp_ref[...], take(q))
+        fetch(q + 2)
+        quads[q].wait()
+
+        def body(at):
+            lows[q, at, :] = (work[at, :] * quad[q, at, :]).astype(jnp.bfloat16)
+
+        chunks(count, body)
+        if q < 3:
+            source = (middle_ref, attended_ref, mlp_ref)[q]
+            quads[q] = pltpu.make_async_copy(source, quad.at[q], quad_sem.at[q])
+            quads[q].start()
+
+    def up_grad(q):
+        put(q, hidden_two_ref, lows.at[q], up_part_ref.at[q])
+
+    def through_up(q):
+        value = product_by_columns(lows[q], take(4 + q))
+        work[...] = work[...] + value if q else value
+        fetch(6 + q)
+
+    def norm_pull(grad, value, inverse):
+        return inverse * (
+            grad
+            - jnp.mean(grad, axis=-1, keepdims=True)
+            - value * jnp.mean(grad * value, axis=-1, keepdims=True)
+        )
+
+    def add_sums(segments, which, value):
+        for crop in range(CROPS):
+            kept = jnp.where(segments == crop, value, 0.0)
+            sums[which, crop] = sums[which, crop] + kept[:8] + kept[8:]
+
+    def second_norm():
+        for q in range(3):
+            quads[q].wait()
+        sums[...] = jnp.zeros_like(sums)
+
+        def body(at):
+            segments = seg_col_ref[at, :1]
+            grad = work[at, :]
+            value, inverse = normed(quad[0, at, :])
+            level = level_ref[3:4, :1]
+            for crop in (2, 1, 0):
+                level = jnp.where(segments == crop, level_ref[crop : crop + 1, :1], level)
+            grad_out = cot_ref[at, :].astype(jnp.float32) * level
+            add_sums(segments, 3, grad)
+            add_sums(segments, 4, grad * value)
+            add_sums(segments, 5, grad_out * quad[2, at, :])
+            scaled = grad * (1.0 + pick(segments, table_ref, 4, 1, width))
+            total = grad_out + norm_pull(scaled, value, inverse)
+            grad_middle[at, :] = total
+            add_sums(segments, 2, total * quad[1, at, :])
+            lows[3, at, :] = (total * pick(segments, table_ref, 0, 2, width)).astype(jnp.bfloat16)
+
+        chunks(count, body)
+
+    def through_out():
+        grad_context[...] = product_by_columns(lows[3], take(8)).astype(jnp.bfloat16)
+        fetch(10)
+        put(4, context_ref, lows.at[3], mixer_part_ref.at[3])
+        for h in (0, 1):
+            same = seg_col_ref[:, :1] == seg_all_ref[h][:1, :]
+            bias[:, h * count : (h + 1) * count] = jnp.where(same, 0.0, LARGE_NEGATIVE)
+
+    def attend_back(first, last):
+        size = width // HEADS
+        scale = 1.0 / math.sqrt(size)
+
+        def body(head, carry):
+            columns, inside = window_of(head, size, width)
+            query, keys = query_ref[:, columns], sides_ref[0, :, columns]
+            grad = grad_context[:, columns]
+            scores = product_by_columns(jnp.where(inside, query, jnp.zeros_like(query)), keys)
+            lane = lax.broadcasted_iota(jnp.int32, (1, 128), 1)
+            total = jnp.sum(jnp.where(lane == head, total_ref[...], 0.0), axis=-1, keepdims=True)
+            chance = jnp.exp(scores * scale + bias[...] - total)
+            pulled = product_by_columns(
+                jnp.where(inside, grad, jnp.zeros_like(grad)), sides_ref[1, :, columns]
+            )
+            inner = jnp.sum(chance * pulled, axis=-1, keepdims=True)
+            grad_scores = (chance * (pulled - inner)).astype(jnp.bfloat16)
+            grad_query = (product(grad_scores, keys) * scale).astype(jnp.bfloat16)
+            lows[0, :, columns] = jnp.where(inside, grad_query, lows[0, :, columns])
+            grad_key = product_by_rows(grad_scores, query) * scale
+            grad_value = product_by_rows(chance.astype(jnp.bfloat16), grad)
+            for h in (0, 1):
+                here = slice(h * count, (h + 1) * count)
+                quad[h, :, columns] = jnp.where(inside, grad_key[here], quad[h, :, columns])
+                quad[2 + h, :, columns] = jnp.where(inside, grad_value[here], quad[2 + h, :, columns])
+            return carry
+
+        lax.fori_loop(first, last, body, 0)
+
+    def swap_sides():
+        for j in (0, 1):
+            leave[j] = quad[2 * j + 1 - c].astype(jnp.bfloat16)
+            send("end", leave.at[j], enter.at[j], side_send.at[j], side_recv.at[j], c_peer)
+
+    def query_grad():
+        put(5, hidden_ref, lows.at[0], mixer_part_ref.at[0])
+
+    def sides_grad():
+        for j in (0, 1):
+            arrive(enter.at[j], side_recv.at[j], c_peer)
+
+            def body(at):
+                total = quad[2 * j + c, at, :] + enter[j, at, :].astype(jnp.float32)
+                lows[1 + j, at, :] = total.astype(jnp.bfloat16)
+
+            chunks(count, body)
+            put(6 + j, hidden_ref, lows.at[1 + j], mixer_part_ref.at[1 + j])
+
+    def through_qkv():
+        for q in range(3):
+            value = product_by_columns(lows[q], take(9 + q))
+            work[...] = work[...] + value if q else value
+            fetch(11 + q)
+
+    def first_norm():
+        def body(at):
+            segments = seg_col_ref[at, :1]
+            grad = work[at, :]
+            value, inverse = normed(tokens_ref[at, :].astype(jnp.float32))
+            add_sums(segments, 0, grad)
+            add_sums(segments, 1, grad * value)
+            scaled = grad * (1.0 + pick(segments, table_ref, 0, 1, width))
+            tokens_grad_ref[at, :] = grad_middle[at, :] + norm_pull(scaled, value, inverse)
+
+        chunks(count, body)
+        for which in range(6):
+            for crop in range(CROPS):
+                row = which // 3 * CROPS + crop
+                columns = slice(which % 3 * width, (which % 3 + 1) * width)
+                sums_row[row : row + 1, columns] = jnp.sum(sums[which, crop], axis=0, keepdims=True)
+        send("end", sums_row, sums_core, m_send, m_recv, c_peer)
+
+    side = sums_row.shape[1]
+
+    def place(k, other_y, other_x):
+        zz = (z - k + 4) % 4
+        yy = 1 - y if other_y else y
+        xx = 1 - x if other_x else x
+        return band.at[c, pl.ds(pl.multiple_of((zz * 4 + yy * 2 + xx) * 8, 8), 8)]
+
+    def sums_start():
+        arrive(sums_core, m_recv, c_peer)
+        near = pl.ds(pl.multiple_of(c * (side - BAND), 128), BAND)
+        band[c, pl.ds(pl.multiple_of(me * 8, 8), 8), :] = sums_row[:, near] + sums_core[:, near]
+        mine = place(0, 0, 0)
+        for k in (1, 2, 3):
+            send("end", mine, mine, mz_send.at[k - 1], mz_recv.at[k - 1], device((z + k) % 4, y, x, c))
+        send("end", mine, mine, mx_send.at[0], mx_recv.at[0], x_peer)
+        send("end", mine, mine, my_send.at[0], my_recv.at[0], y_peer)
+
+    def sums_line():
+        for k in (1, 2, 3):
+            piece = place(k, 0, 0)
+            arrive(piece, mz_recv.at[k - 1], device((z - k + 4) % 4, y, x, c))
+            send("end", piece, piece, mx_send.at[k], mx_recv.at[k], x_peer)
+            send("end", piece, piece, my_send.at[k], my_recv.at[k], y_peer)
+
+    def sums_plane():
+        for k in range(4):
+            from_side, from_up = place(k, 0, 1), place(k, 1, 0)
+            arrive(from_side, mx_recv.at[k], x_peer)
+            arrive(from_up, my_recv.at[k], y_peer)
+            if k % 2:
+                send("end", from_side, from_side, md_send.at[k], md_recv.at[k], y_peer)
+            else:
+                send("end", from_up, from_up, md_send.at[k], md_recv.at[k], x_peer)
+
+    def sums_cores():
+        for k in range(4):
+            arrive(place(k, 1, 1), md_recv.at[k], y_peer if k % 2 else x_peer)
+        send("end", band.at[c], band.at[c], mc_send, mc_recv, c_peer)
+
+    def condition():
+        arrive(band.at[1 - c], mc_recv, c_peer)
+        acts = conds_ref[:, :8, :].astype(jnp.float32).reshape(CHIPS * 8, 128)
+        row = lax.broadcasted_iota(jnp.int32, acts.shape, 0) % 8
+        acts = jnp.where(row < CROPS, acts, 0.0)
+        upper = acts.astype(jnp.bfloat16)
+        lower = pltpu.roll(acts, CROPS, 0).astype(jnp.bfloat16)
+        sides = [jnp.zeros((CHIPS * 8, 128), jnp.float32)] * 2
+        for at, source, skip, size in ((0, 0, 0, BAND), (BAND, 1, 2 * BAND - side, side - BAND)):
+            terms = split_low(band[source, :, skip : skip + size])
+            for which, act in enumerate((upper, lower)):
+                columns = slice(which * side + at, which * side + at + size)
+                value = product_by_rows(act, terms[0]) + product_by_rows(act, terms[1])
+                ada_grad_ref[:, columns] = value[:share]
+                for term in terms:
+                    sides[which] = sides[which] + product_by_columns(term, ada_ref[:, columns])
+        silu_part[...] = sides[0] + pltpu.roll(sides[1], CHIPS * 8 - CROPS, 0)
+        silu_ref[c, me] = silu_part[pl.ds(pl.multiple_of(me * 8, 8), 8), :]
+        for k in range(1, CHIPS):
+            to = (me + k) % CHIPS
+            src = silu_part.at[pl.ds(pl.multiple_of(to * 8, 8), 8)]
+            send("end", src, silu_ref.at[c, me], s_send.at[k - 1], s_recv.at[k - 1], (to, c))
+
+    def condition_cores():
+        for k in range(1, CHIPS):
+            source = (me - k + CHIPS) % CHIPS
+            arrive(silu_ref.at[c, source], s_recv.at[k - 1], (source, c))
+        send("end", silu_ref.at[c], silu_ref.at[c], sc_send, sc_recv, c_peer)
+
+    extra = {
+        0: [partial(through_down, 0), partial(through_down, 1)],
+        1: [partial(through_down, 2), partial(through_down, 3), partial(up_grad, 0)],
+        2: [partial(up_grad, 1), partial(up_grad, 2), partial(up_grad, 3)],
+        3: [partial(through_up, q) for q in range(4)] + [second_norm],
+        4: [through_out, partial(attend_back, 0, 4)],
+        5: [partial(attend_back, 4, 12)],
+        6: [partial(attend_back, 12, 16), swap_sides, query_grad, sides_grad],
+        7: [through_qkv, first_norm],
+        8: [sums_start],
+        9: [sums_line],
+        10: [sums_plane],
+        11: [sums_cores],
+        12: [condition],
+        13: [condition_cores],
+    }
+    begin(0)
+    for q in range(4):
+        slopes(q)
+    fetch(0)
+    fetch(1)
     for i in range(len(order) + 2):
-        if i + 3 < len(order):
-            begin(*order[i + 3])
+        if i + 1 < len(order):
+            if (i + 1) % 4 == 0:
+                for n in sorted(going):
+                    going.pop(n).wait()
+            begin(i + 1)
         if i < len(order):
-            pair(*order[i])
+            pair(i)
         if 1 <= i < len(order) + 1:
-            relay(*order[i - 1])
+            relay(i - 1)
         if 2 <= i:
-            plane(*order[i - 2])
+            plane(i - 2)
+        for step in extra.get(i, ()):
+            step()
     for a in range(2):
         for j, (px, pc) in enumerate(partners):
             arrive(rows_ref.at[a, px * 2 + pc], group_recv.at[a, j], device(z, y, px, pc))
-    for copy in sends:
-        copy.wait_send()
-
-
-def scatter_grads(first, second, third, share):
-    rows, width = third.shape[-2:]
+    arrive(silu_ref.at[1 - c], sc_recv, c_peer)
+    for owner in list(sends):
+        finish_sends(owner)
+
+
+def run_backward(given, share):
+    (weights, down_part, slope, middle, attended, mlp, hidden, query, sides, total, context, hidden_two,
+     grad_mlp, table, conds, level, seg_all, seg_col, tokens, cot, ada) = given
+    count, width = tokens.shape
+    rows, side = 4 * share, ada.shape[1] // 2
     dma = pltpu.SemaphoreType.DMA
-    low = jnp.bfloat16
+    low, wide = jnp.bfloat16, jnp.float32
+    vmem, any_ = pl.BlockSpec(memory_space=pltpu.VMEM), pl.BlockSpec(memory_space=pl.ANY)
+    out, buffer = jax.ShapeDtypeStruct, pltpu.VMEM
+    slots = 12
     return pl.pallas_call(
-        partial(scatter_kernel, share),
+        partial(backward_kernel, share),
         out_shape=(
-            jax.ShapeDtypeStruct((2, 4, PAD, width), low),
-            jax.ShapeDtypeStruct((rows, width), jnp.float32),
+            out((4, width, width), low),
+            out((4, width, width), low),
+            out((2, 4, PAD, width), low),
+            out((rows, width), wide),
+            out((count, width), wide),
+            out((share, ada.shape[1]), wide),
+            out((2, CHIPS, 8, 128), wide),
         ),
-        in_specs=[pl.BlockSpec(memory_space=pl.ANY)] * 3,
-        out_specs=[pl.BlockSpec(memory_space=pltpu.VMEM)] * 2,
+        in_specs=[any_] * 6 + [vmem] * 15,
+        out_specs=[any_] * 2 + [vmem] * 5,
         scratch_shapes=[
-            pltpu.VMEM((3, 4, 4, rows, width), low),
-            pltpu.VMEM((3, 4, 4, rows, width), low),
-            pltpu.VMEM((3, 4, rows, width), low),
-            pltpu.VMEM((3, 4, rows, width), low),
-            pltpu.VMEM((3, 4, rows, width), low),
-            pltpu.VMEM((3, 3, rows, width), low),
-            pltpu.VMEM((2, 4 * PAD, width), low),
-            dma((3, 4, 4)), dma((3, 4, 4)), dma((3, 4, 4)),
-            dma((3, 4)), dma((3, 4)), dma((3, 4)), dma((3, 4)),
-            dma((3, 4, 2)), dma((3, 4, 2)), dma((3, 4, 2)), dma((3, 4, 2)),
-            dma((3, 3)), dma((3, 3)), dma((2, 3)), dma((2, 3)),
+            buffer((5, 4, rows, width), low),
+            buffer((4, 4, rows, width), low),
+            buffer((4, rows, width), low),
+            buffer((5, rows, width), low),
+            buffer((5, rows, width), low),
+            buffer((3, 3, rows, width), low),
+            buffer((2, 4 * PAD, width), low),
+            buffer((2, width, width), low),
+            buffer((2, width, width), low),
+            buffer((4, count, width), wide),
+            buffer((4, count, width), low),
+            buffer((count, width), wide),
+            buffer((count, width), wide),
+            buffer((count, width), low),
+            buffer((2, count, width), low),
+            buffer((2, count, width), low),
+            buffer((count, 2 * count), wide),
+            buffer((6, CROPS, 8, width), wide),
+            buffer((8, side), wide),
+            buffer((8, side), wide),
+            buffer((2, CHIPS * 8, BAND), wide),
+            buffer((CHIPS * 8, 128), wide),
+            dma((slots, 4)), dma((slots, 4)), dma((slots, 4)),
+            dma((slots,)), dma((slots,)), dma((slots,)), dma((slots,)),
+            dma((slots, 2)), dma((slots, 2)), dma((slots, 2)), dma((slots, 2)),
+            dma((3, 3)), dma((3, 3)), dma((2, 3)), dma((2, 3)), dma((2,)), dma((2,)), dma((4,)),
+            dma((2,)), dma((2,)), dma, dma, dma((3,)), dma((3,)), dma((4,)), dma((4,)), dma((4,)), dma((4,)),
+            dma((4,)), dma((4,)), dma, dma, dma((CHIPS - 1,)), dma((CHIPS - 1,)), dma, dma,
         ],
         compiler_params=pltpu.CompilerParams(
-            collective_id=1, has_side_effects=True, vmem_limit_bytes=58 * 2**20
+            collective_id=1, has_side_effects=True, vmem_limit_bytes=63 * 2**20
         ),
-        name="scatter_grads",
-    )(first, second, third)
+        name="backward",
+    )(*given)
 
 
 def layer_norm(values):
@@ -818,6 +1127,87 @@
     )
 
 
+def layer_plain(tokens_float, segments, conditions, noise_bins, bin_counts, cotangent, ada_weight, first,
+                up_weight, down_weight):
+    width = tokens_float.shape[1]
+    (
+        (mixers, uppers, downers), activated, slope, hidden_one, queries, sides, log_total,
+        context_low, attended, middle, hidden_two, mlp_out, modulation, cond_act, crop_weight, same_crop,
+    ) = forward_plain(
+        tokens_float, segments, conditions, noise_bins, bin_counts, ada_weight, first, up_weight,
+        down_weight,
+    )
+    selector = (segments[:, None] == jnp.arange(CROPS, dtype=jnp.int32)).astype(jnp.float32)
+    per_token = jnp.einsum("tc,cf->tf", selector, modulation, precision=lax.Precision.HIGHEST)
+    _, scale_one, gate_one, _, scale_two, gate_two = jnp.split(per_token, 6, axis=-1)
+    normed_one, inverse_one = layer_norm(tokens_float)
+    normed_two, inverse_two = layer_norm(middle)
+
+    token_weight = jnp.sum(selector * crop_weight[None, :], axis=-1)
+    grad_out = cotangent.astype(jnp.float32) * token_weight[:, None]
+    grad_mlp = (grad_out * gate_two).astype(jnp.bfloat16)
+    tokens_out = (middle + gate_two * mlp_out).astype(jnp.bfloat16)
+    down_part = dots("qtf,td->qfd", activated, grad_mlp).astype(jnp.bfloat16)
+    grad_act = dots("td,qfd->qtf", grad_mlp, downers)
+    grad_upper = (grad_act * slope).astype(jnp.bfloat16)
+    up_part = dots("td,qtf->qdf", hidden_two, grad_upper).astype(jnp.bfloat16)
+    grad_hidden_two = dots("qtf,qdf->td", grad_upper, uppers)
+    grad_middle = grad_out + norm_back(grad_hidden_two * (1.0 + scale_two), normed_two, inverse_two)
+    grad_attended = (grad_middle * gate_one).astype(jnp.bfloat16)
+    grad_context = dots("tf,df->td", grad_attended, mixers[3]).astype(jnp.bfloat16)
+    grad_query, grad_key, grad_value = attend_back(
+        queries, sides[0], sides[1], same_crop, log_total, grad_context
+    )
+    grad_sides = lax.psum_scatter(
+        jnp.stack([grad_key, grad_value]).astype(jnp.bfloat16),
+        "sp",
+        scatter_dimension=1,
+        tiled=True,
+    )
+    grad_projected = jnp.concatenate([grad_query.astype(jnp.bfloat16)[None], grad_sides])
+    out_part = dots("td,tf->df", context_low, grad_attended).astype(jnp.bfloat16)
+    qkv_part = dots("td,qtf->qdf", hidden_one, grad_projected).astype(jnp.bfloat16)
+    first_part = jnp.concatenate([qkv_part, out_part[None]])
+    grad_hidden_one = dots("qtf,qdf->td", grad_projected, mixers[:3])
+    tokens_grad = grad_middle + norm_back(
+        grad_hidden_one * (1.0 + scale_one), normed_one, inverse_one
+    )
+
+    joined = jnp.stack([first_part, up_part]).transpose(2, 0, 1, 3).reshape(width, 8 * width)
+    rows = lax.psum_scatter(joined, ("dp", "sp"), scatter_dimension=0, tiled=True)
+    rows = rows.astype(jnp.float32)
+    first_grad, up_grad = rows[:, : 4 * width], rows[:, 4 * width :]
+    down_grad = lax.psum_scatter(
+        down_part.reshape(4 * width, width), ("dp", "sp"), scatter_dimension=0, tiled=True
+    ).astype(jnp.float32)
+
+    grad_per_token = jnp.concatenate(
+        [
+            grad_hidden_one,
+            grad_hidden_one * normed_one,
+            grad_middle * attended,
+            grad_hidden_two,
+            grad_hidden_two * normed_two,
+            grad_out * mlp_out,
+        ],
+        axis=-1,
+    )
+    grad_modulation = lax.psum(
+        jnp.einsum("tc,tf->cf", selector, grad_per_token, precision=lax.Precision.HIGHEST), "sp"
+    )
+    grad_rows = lax.all_gather(grad_modulation, "dp", axis=0, tiled=True)
+    ada_grad = jnp.einsum(
+        "sd,sf->df", cond_act.astype(jnp.float32), grad_rows, precision=lax.Precision.HIGHEST
+    )
+    silu_part = jnp.einsum(
+        "sf,df->sd", grad_rows, ada_weight.astype(jnp.float32), precision=lax.Precision.HIGHEST
+    )
+    silu_all = lax.all_gather(silu_part, ("dp", "sp"), axis=0)
+    silu_here = lax.dynamic_slice_in_dim(silu_all, lax.axis_index("dp") * CROPS, CROPS, axis=1)
+    grad_silu = silu_here.transpose(1, 0, 2).reshape(CROPS, width)
+    return tokens_out, tokens_grad, grad_silu, ada_grad, first_grad, up_grad, down_grad
+
+
 def on_device(
     chips,
     tokens_in,
@@ -844,102 +1234,24 @@
         )
         (
             weights, down_part, slope, hidden_one, queries, sides, log_total, context_low, attended,
-            middle, hidden_two, mlp_out, tokens_out, table, conds, level,
+            middle, hidden_two, mlp_out, tokens_out, table, conds, level, grad_mlp, seg_all,
         ) = run_forward(
             shards, down_weight, acts, ada, tokens_in[0], cotangent[0], seg_col, seg_row, bins, share
         )
-        mixers, uppers, downers = weights[0], weights[1], weights[2]
-        modulation = jnp.concatenate([table[:CROPS], table[CROPS:]], axis=1)
-        cond_act = conds[:, :CROPS, :share].reshape(-1, share)
-        crop_weight = level[:CROPS, 0]
-        log_total = log_total[:, :HEADS].T
-        all_segments = lax.all_gather(segments, "sp", axis=0, tiled=True)
-        same_crop = segments[:, None] == all_segments[None, :]
-    else:
-        (
-            (mixers, uppers, downers), activated, slope, hidden_one, queries, sides, log_total,
-            context_low, attended, middle, hidden_two, mlp_out, modulation, cond_act, crop_weight, same_crop,
-        ) = forward_plain(
-            tokens_float, segments, conditions[0], noise_bins[0], bin_counts[0], ada_weight, first,
-            up_weight, down_weight,
+        given = (
+            weights, down_part, slope, middle, attended, mlp_out, hidden_one, queries, sides, log_total,
+            context_low, hidden_two, grad_mlp, table, conds, level, seg_all, seg_col, tokens_in[0],
+            cotangent[0], ada,
         )
-    selector = (segments[:, None] == jnp.arange(CROPS, dtype=jnp.int32)).astype(jnp.float32)
-    per_token = jnp.einsum("tc,cf->tf", selector, modulation, precision=lax.Precision.HIGHEST)
-    _, scale_one, gate_one, _, scale_two, gate_two = jnp.split(per_token, 6, axis=-1)
-    normed_one, inverse_one = layer_norm(tokens_float)
-    normed_two, inverse_two = layer_norm(middle)
-
-    token_weight = jnp.sum(selector * crop_weight[None, :], axis=-1)
-    grad_out = cotangent[0].astype(jnp.float32) * token_weight[:, None]
-    grad_mlp = (grad_out * gate_two).astype(jnp.bfloat16)
-    if not kernels:
-        tokens_out = (middle + gate_two * mlp_out).astype(jnp.bfloat16)
-        down_part = dots("qtf,td->qfd", activated, grad_mlp).astype(jnp.bfloat16)
-    grad_act = dots("td,qfd->qtf", grad_mlp, downers)
-    grad_upper = (grad_act * slope).astype(jnp.bfloat16)
-    up_part = dots("td,qtf->qdf", hidden_two, grad_upper).astype(jnp.bfloat16)
-    grad_hidden_two = dots("qtf,qdf->td", grad_upper, uppers)
-    grad_middle = grad_out + norm_back(grad_hidden_two * (1.0 + scale_two), normed_two, inverse_two)
-    grad_attended = (grad_middle * gate_one).astype(jnp.bfloat16)
-    grad_context = dots("tf,df->td", grad_attended, mixers[3]).astype(jnp.bfloat16)
-    grad_query, grad_key, grad_value = attend_back(
-        queries, sides[0], sides[1], same_crop, log_total, grad_context
-    )
-    grad_sides = lax.psum_scatter(
-        jnp.stack([grad_key, grad_value]).astype(jnp.bfloat16),
-        "sp",
-        scatter_dimension=1,
-        tiled=True,
-    )
-    grad_projected = jnp.concatenate([grad_query.astype(jnp.bfloat16)[None], grad_sides])
-    out_part = dots("td,tf->df", context_low, grad_attended).astype(jnp.bfloat16)
-    qkv_part = dots("td,qtf->qdf", hidden_one, grad_projected).astype(jnp.bfloat16)
-    first_part = jnp.concatenate([qkv_part, out_part[None]])
-    grad_hidden_one = dots("qtf,qdf->td", grad_projected, mixers[:3])
-    tokens_grad = grad_middle + norm_back(
-        grad_hidden_one * (1.0 + scale_one), normed_one, inverse_one
-    )
-
-    if kernels:
-        pieces = (32, 4 * share, width)
-        rows, down_grad = scatter_grads(
-            first_part.reshape(pieces), up_part.reshape(pieces), down_part.reshape(pieces), share
-        )
+        _, _, rows, down_grad, tokens_grad, ada_grad, silu_part = run_backward(given, share)
         rows = rows[:, :, :share].astype(jnp.float32).transpose(0, 2, 1, 3).reshape(2, share, 4 * width)
         first_grad, up_grad = rows[0], rows[1]
+        grad_silu = silu_part[:, :, :CROPS, :share].transpose(2, 1, 0, 3).reshape(CROPS, width)
     else:
-        joined = jnp.stack([first_part, up_part]).transpose(2, 0, 1, 3).reshape(width, 8 * width)
-        rows = lax.psum_scatter(joined, ("dp", "sp"), scatter_dimension=0, tiled=True)
-        rows = rows.astype(jnp.float32)
-        first_grad, up_grad = rows[:, : 4 * width], rows[:, 4 * width :]
-        down_grad = lax.psum_scatter(
-            down_part.reshape(4 * width, width), ("dp", "sp"), scatter_dimension=0, tiled=True
-        ).astype(jnp.float32)
-
-    grad_per_token = jnp.concatenate(
-        [
-            grad_hidden_one,
-            grad_hidden_one * normed_one,
-            grad_middle * attended,
-            grad_hidden_two,
-            grad_hidden_two * normed_two,
-            grad_out * mlp_out,
-        ],
-        axis=-1,
-    )
-    grad_modulation = lax.psum(
-        jnp.einsum("tc,tf->cf", selector, grad_per_token, precision=lax.Precision.HIGHEST), "sp"
-    )
-    grad_rows = lax.all_gather(grad_modulation, "dp", axis=0, tiled=True)
-    ada_grad = jnp.einsum(
-        "sd,sf->df", cond_act.astype(jnp.float32), grad_rows, precision=lax.Precision.HIGHEST
-    )
-    silu_part = jnp.einsum(
-        "sf,df->sd", grad_rows, ada_weight.astype(jnp.float32), precision=lax.Precision.HIGHEST
-    )
-    silu_all = lax.all_gather(silu_part, ("dp", "sp"), axis=0)
-    silu_here = lax.dynamic_slice_in_dim(silu_all, lax.axis_index("dp") * CROPS, CROPS, axis=1)
-    grad_silu = silu_here.transpose(1, 0, 2).reshape(CROPS, width)
+        tokens_out, tokens_grad, grad_silu, ada_grad, first_grad, up_grad, down_grad = layer_plain(
+            tokens_float, segments, conditions[0], noise_bins[0], bin_counts[0], cotangent[0],
+            ada_weight, first, up_weight, down_weight,
+        )
     silu_pull = jax.vjp(jax.nn.silu, conditions[0].astype(jnp.float32))[1]
     cond_grad = silu_pull(grad_silu)[0]
     return (

time: 572 us -> 392 us (0.69)
  the two profiles are of different devices: /device:TPU:0 before, /device:TPU:9 now
where the time goes in v1:
time: 392 us; the launch traced here: 384 us
  Pallas kernels  362 us (92%)
  local copies, waits for them, and re-layouts  17.7 us (5%)
    pallas_call x1, Pallas kernels, run_forward(): pl.pallas_call(partial(forward_kernel, share), out_shape=(out((3, 4, widt...  184 us
    pallas_call x1, Pallas kernels, run_backward(): pl.pallas_call(partial(backward_kernel, share), out_shape=(out((4, width,...  178 us

profile of v1, /device:TPU:9, one launch (start us, length us, event | category | flops | bytes accessed | tf_op | source)
XLA Modules:
  0.0 384.1 jit_solution(4255232751913382212)
XLA Ops:
  0.7 0.7 pad.29
  1.4 0.7 convert_bitcast_fusion.1
  2.0 0.7 fusion.4.bins_ref
  2.7 1.3 broadcast_in_dim.27.seg_row_ref
  4.0 0.8 reshape.38
  5.0 0.6 pad.27.act_ref
  5.6 1.4 broadcast_in_dim.26.seg_col_ref
  7.0 1.1 stack.10
  8.5 1.0 pad.24.shards_ref
  9.5 1.4 pad.28.ada_ref
  10.9 184.1 %forward.1 = (bf16[3,4,1152,1152]{3,2,1,0:T(8,128)(2,1)}, bf16[4,1152,1152]{2,1,0:T(8,128)(2,1)}, f32[4,256,1152]{2,1,0:T(8,128)}, bf16[256,1152]{1,0:T(8,128)(2...) custom-call(bf16[2,4,48,1152]{3,2,1,0:T(8,128)(2,1)} %pad.24.shards_, ...), custom_call_target="tpu_custom_call" | custom-call | tf_op jit(solution)/shard_map/forward/pallas_call | solution.py:464
  195.0 177.5 %backward.1 = (bf16[4,1152,1152]{2,1,0:T(8,128)(2,1)}, bf16[4,1152,1152]{2,1,0:T(8,128)(2,1)}, bf16[2,4,48,1152]{3,2,1,0:T(8,128)(2,1)}, f32[144,1152]{1,0:T(8,1...) custom-call(bf16[3,4,1152,1152]{3,2,1,0:T(8,128)(2,1)} %get-tuple-element.32.weights_ref, ...), custom_call_target="tpu_custom_call" | custom-call | tf_op jit(solution)/shard_map/backward/pallas_call | solution.py:951
  372.6 0.9 slice_bitcast_fusion
  373.7 0.6 fusion.3
  374.4 1.2 convert_bitcast_fusion
  376.2 0.9 copy.44
  377.3 0.7 slice.28
  378.0 0.8 slice.27
  378.8 0.8 copy.54
  379.6 1.0 copy.55
  380.6 0.7 copy-done.1
  381.3 1.0 copy.56
  382.3 0.5 copy-done.2
  382.8 0.8 copy.57
  (32 shorter events, 1.4 us)
Async XLA Ops:
  0.6 7.6 %copy-start.6 = (bf16[36,1152]{1,0:T(8,128)(2,1)S(1)}, bf16[36,1152]{1,0:T(8,128)(2,1)}, u32[]{:S(2)}) copy-start(bf16[36,1152]{1,0:T(8,128)(2,1)} %param.19) | copy-start | bytes 248836
  0.6 7.6 %copy-start.5 = (bf16[36,3456]{1,0:T(8,128)(2,1)S(1)}, bf16[36,3456]{1,0:T(8,128)(2,1)}, u32[]{:S(2)}) copy-start(bf16[36,3456]{1,0:T(8,128)(2,1)} %param.18) | copy-start | bytes 746500
  8.4 1.1 copy-start.4
  195.0 178.7 %copy-start.7 = (bf16[1,4,1152]{2,1,0:T(4,128)(2,1)S(1)}, bf16[1,4,1152]{2,1,0:T(4,128)(2,1)}, u32[]{:S(2)}) copy-start(bf16[1,4,1152]{2,1,0:T(4,128)(2,1)} %param.13) | copy-start | bytes 27652
  377.2 1.6 copy-start.3
  377.3 2.4 copy-start
  379.6 1.7 copy-start.1
  381.3 1.5 copy-start.2
